TPU v7x, 512 devices: a whole 4x8x8 slice. The times are simulated.
512 devices in a mesh: depth: 8 (over y), plane: 64 (over x, z, core).
Axes of the slice: x: 4, y: 8, z: 8, core: 2. Of those that a mesh axis runs over, the one named last changes fastest.
Arguments:
- populations: float32 [8, 256, 19, 4096], P('depth', 'plane'), may hold values from 0.5 to 1.5
- fluid_mask: int32 [8, 256, 4096], P('depth', 'plane'), may hold values 0 or 1
- block_per_slot: int32 [256], replicated, may hold values from 0 to 128, as said below
- neighbours: int32 [128, 4], replicated, may hold values from 0 to 127, as said below
Outputs:
- evolved: float32 [8, 256, 19, 4096], P('depth', 'plane')
Inputs may be any that keep to these rules, and one draw needn't show every extreme that they name: `block_per_slot`: each of the 128 blocks stands in exactly one slot; slots p * 4 to p * 4 + 3 belong to device p of the layer, its blocks first and then empty slots holding 128; every device holds 1 to 4 blocks and some device exactly 4. `neighbours`: the blocks form a periodic grid of 16 by 8; each row names the four blocks beside it in that grid.
All inputs are finite; a program needn't handle non-finite values. No bound on the sum of `fluid_mask` on one device may be relied on, other than what follows from the above.
Results may differ from a plain program's by a relative error of at most 0.0003.
Values sent between devices are 32-bit elements; how exact they have to be, the bound alone decides.
A program may use at most 128 MiB of HBM per device.

v0:
```python
import jax
import jax.numpy as jnp
import numpy as np
from jax import lax
from jax.sharding import PartitionSpec as P

BE = 16
STEPS = 2


lattice_dirs = [
    (0, 0, 0),
    (1, 0, 0),
    (-1, 0, 0),
    (0, 1, 0),
    (0, -1, 0),
    (0, 0, 1),
    (0, 0, -1),
    (1, 1, 0),
    (-1, -1, 0),
    (1, -1, 0),
    (-1, 1, 0),
    (1, 0, 1),
    (-1, 0, -1),
    (1, 0, -1),
    (-1, 0, 1),
    (0, 1, 1),
    (0, -1, -1),
    (0, 1, -1),
    (0, -1, 1),
]
opposite_dirs = [0, 2, 1, 4, 3, 6, 5, 8, 7, 10, 9, 12, 11, 14, 13, 16, 15, 18, 17]
xplus_dirs = [1, 7, 9, 11, 13]
xminus_dirs = [2, 8, 10, 12, 14]
positive_y_directions = [3, 7, 10, 15, 17]
yminus_dirs = [4, 8, 9, 16, 18]
zplus_dirs = [5, 11, 14, 15, 18]
zminus_dirs = [6, 12, 13, 16, 17]
relax_rates = [
    0.0,
    1.19,
    1.4,
    0.0,
    1.2,
    0.0,
    1.2,
    0.0,
    1.2,
    1.25,
    1.4,
    1.25,
    1.4,
    1.25,
    1.25,
    1.25,
    1.98,
    1.98,
    1.98,
]
table_order = (0, 1, 2, 3, 0, 1, 0, 1)


def passed_along(block, axis, distance):
    devices = range(lax.axis_size(axis))
    route = [((i - distance) % len(devices), i) for i in devices]
    return lax.ppermute(block, axis, route)


def weight_column():
    values = [1.0 / 3.0] + [1.0 / 18.0] * 6 + [1.0 / 36.0] * 12
    return jnp.asarray(np.array(values), jnp.float32)[:, None]


def moment_tables():
    velo = np.array(lattice_dirs) * 1.0
    cxv, cyv, czv = (velo[:, 0], velo[:, 1], velo[:, 2])
    csq = cxv * cxv + cyv * cyv + czv * czv
    rows = [
        np.ones(19),
        19.0 * csq - 30.0,
        (21.0 * csq * csq - 53.0 * csq + 24.0) / 2.0,
        cxv,
        (5.0 * csq - 9.0) * cxv,
        cyv,
        (5.0 * csq - 9.0) * cyv,
        czv,
        (5.0 * csq - 9.0) * czv,
        3.0 * cxv * cxv - csq,
        (3.0 * csq - 5.0) * (3.0 * cxv * cxv - csq),
        cyv * cyv - czv * czv,
        (3.0 * csq - 5.0) * (cyv * cyv - czv * czv),
        cxv * cyv,
        cyv * czv,
        cxv * czv,
        (cyv * cyv - czv * czv) * cxv,
        (czv * czv - cxv * cxv) * cyv,
        (cxv * cxv - cyv * cyv) * czv,
    ]
    matrix = np.stack(rows)
    inverse = matrix.T / np.sum(matrix * matrix, axis=1)[None, :]
    relax = inverse * np.array(relax_rates)[None, :]
    return (jnp.asarray(matrix, jnp.float32), jnp.asarray(relax, jnp.float32))


def collide(population_field, fluid):
    matrix, relax = moment_tables()
    moments = jnp.einsum("qi,sic->sqc", matrix, population_field, precision=lax.Precision.HIGHEST)
    rho = moments[:, 0]
    jxv = moments[:, 3]
    jyv = moments[:, 5]
    jzv = moments[:, 7]
    jsq = jxv * jxv + jyv * jyv + jzv * jzv
    pxx = 2.0 * jxv * jxv - jyv * jyv - jzv * jzv
    pww = jyv * jyv - jzv * jzv
    empty_population = jnp.zeros_like(rho)
    equilibrium = jnp.stack(
        [
            rho,
            -11.0 * rho + 19.0 * jsq,
            3.0 * rho - 5.5 * jsq,
            jxv,
            -2.0 / 3.0 * jxv,
            jyv,
            -2.0 / 3.0 * jyv,
            jzv,
            -2.0 / 3.0 * jzv,
            pxx,
            -0.5 * pxx,
            pww,
            -0.5 * pww,
            jxv * jyv,
            jyv * jzv,
            jxv * jzv,
            empty_population,
            empty_population,
            empty_population,
        ],
        axis=1,
    )
    relaxed = population_field - jnp.einsum(
        "qi,sic->sqc", relax, moments - equilibrium, precision=lax.Precision.HIGHEST
    )
    bounced = population_field[:, np.array(opposite_dirs), :]
    return jnp.where(fluid[:, None, :] == 1, relaxed, bounced)


def rims(post):
    slots = post.shape[0]
    cells = post.reshape(slots, 19, BE, BE, BE)
    top_layer = cells[:, np.array(zplus_dirs)][..., BE - 1].reshape(slots, 5, BE * BE)
    bottom_layer = cells[:, np.array(zminus_dirs)][..., 0].reshape(slots, 5, BE * BE)
    return (top_layer, bottom_layer)


def extend_depth(post, lower_rim, upper_rim):
    slots = post.shape[0]
    cells = post.reshape(slots, 19, BE, BE, BE)
    lower = (
        jnp.zeros((slots, 19, BE, BE), jnp.float32)
        .at[:, np.array(zplus_dirs)]
        .set(lower_rim.reshape(slots, 5, BE, BE))
    )
    upper = (
        jnp.zeros((slots, 19, BE, BE), jnp.float32)
        .at[:, np.array(zminus_dirs)]
        .set(upper_rim.reshape(slots, 5, BE, BE))
    )
    return jnp.concatenate([lower[..., None], cells, upper[..., None]], axis=-1)


def faces(padded):
    slots = padded.shape[0]
    width = BE * (BE + 2)
    xplus = padded[:, np.array(xplus_dirs)][:, :, BE - 1].reshape(slots, 5, width)
    xminus = padded[:, np.array(xminus_dirs)][:, :, 0].reshape(slots, 5, width)
    yplus = padded[:, np.array(positive_y_directions)][:, :, :, BE - 1].reshape(slots, 5, width)
    yminus = padded[:, np.array(yminus_dirs)][:, :, :, 0].reshape(slots, 5, width)
    return (xplus, xminus, yplus, yminus)


def source_slots(my_blocks, block_per_slot, neighbours):
    block_total = neighbours.shape[0]
    slot_total = block_per_slot.shape[0]
    slot_lookup = (
        jnp.zeros((block_total,), jnp.int32)
        .at[block_per_slot]
        .set(jnp.arange(slot_total, dtype=jnp.int32), mode="drop")
    )
    blocks = jnp.minimum(my_blocks, block_total - 1)
    near = neighbours[blocks]
    return jnp.stack(
        [
            slot_lookup[near[:, 0]],
            slot_lookup[near[:, 1]],
            slot_lookup[near[:, 2]],
            slot_lookup[near[:, 3]],
            slot_lookup[neighbours[near[:, 0], 2]],
            slot_lookup[neighbours[near[:, 1], 3]],
            slot_lookup[neighbours[near[:, 0], 3]],
            slot_lookup[neighbours[near[:, 1], 2]],
        ],
        axis=0,
    )


def gather_layers(block_z, xp_in, xm_in, yp_in, ym_in, corner_a, corner_b, corner_c, corner_d):
    ext = jnp.pad(block_z, ((0, 0), (1, 1), (1, 1), (0, 0)))
    ext = ext.at[np.array(xplus_dirs), 0, 1 : BE + 1, :].set(xp_in)
    ext = ext.at[np.array(xminus_dirs), BE + 1, 1 : BE + 1, :].set(xm_in)
    ext = ext.at[np.array(positive_y_directions), 1 : BE + 1, 0, :].set(yp_in)
    ext = ext.at[np.array(yminus_dirs), 1 : BE + 1, BE + 1, :].set(ym_in)
    ext = ext.at[7, 0, 0, :].set(corner_a)
    ext = ext.at[8, BE + 1, BE + 1, :].set(corner_b)
    ext = ext.at[9, 0, BE + 1, :].set(corner_c)
    ext = ext.at[10, BE + 1, 0, :].set(corner_d)
    pieces = []
    for which in range(19):
        cxv, cyv, czv = lattice_dirs[which]
        pieces.append(
            ext[which, 1 - cxv : 1 - cxv + BE, 1 - cyv : 1 - cyv + BE, 1 - czv : 1 - czv + BE]
        )
    return jnp.stack(pieces).reshape(19, BE * BE * BE)


def finish(padded, picked):
    slots = padded.shape[0]
    shaped = [piece.reshape(slots, 5, BE, BE + 2) for piece in picked]
    corner_a = shaped[4][:, 1, BE - 1, :]
    corner_b = shaped[5][:, 1, 0, :]
    corner_c = shaped[6][:, 2, 0, :]
    corner_d = shaped[7][:, 2, BE - 1, :]
    return jax.vmap(gather_layers)(
        padded, shaped[0], shaped[1], shaped[2], shaped[3], corner_a, corner_b, corner_c, corner_d
    )


def shards(populations, fluid_mask, block_per_slot, neighbours):
    column = weight_column()
    population_field = populations[0] * column
    fluid = fluid_mask[0]
    capacity = population_field.shape[0]
    first_slot = lax.axis_index("plane") * capacity
    my_blocks = lax.dynamic_slice_in_dim(block_per_slot, first_slot, capacity)
    sources = source_slots(my_blocks, block_per_slot, neighbours)
    for repeat in range(STEPS):
        post = collide(population_field, fluid)
        top_layer, bottom_layer = rims(post)
        lower_rim = passed_along(top_layer, "depth", 1)
        upper_rim = passed_along(bottom_layer, "depth", -1)
        padded = extend_depth(post, lower_rim, upper_rim)
        xplus, xminus, yplus, yminus = faces(padded)
        tables = (
            lax.all_gather(xplus, "plane", axis=0, tiled=True),
            lax.all_gather(xminus, "plane", axis=0, tiled=True),
            lax.all_gather(yplus, "plane", axis=0, tiled=True),
            lax.all_gather(yminus, "plane", axis=0, tiled=True),
        )
        picked = [
            jnp.take(tables[table_order[which]], sources[which], axis=0) for which in range(8)
        ]
        population_field = finish(padded, list(picked))
    valid = my_blocks < neighbours.shape[0]
    population_field = jnp.where(valid[:, None, None], population_field, 0.0)
    return (population_field / column)[None]


def solution(mesh):
    return jax.shard_map(
        shards,
        mesh=mesh,
        in_specs=(P("depth", "plane", None, None), P("depth", "plane", None), P(), P()),
        out_specs=P("depth", "plane", None, None),
        check_vma=False,
    )
```

profile of v0, /device:TPU:1, one launch (start us, length us, event | category | flops | bytes accessed | tf_op | source)
XLA Modules:
  0.0 1431.5 jit_solution(13953888728943829306)
XLA Ops:
  20.3 4.8 fusion.1
  26.0 7.4 reshape.474
  33.4 4.5 gather_fusion.2
  38.8 5.9 collective-permute-start.1
  44.8 4.5 gather_fusion.1
  52.9 3.8 collective-permute-done
  57.6 8.9 copy.263
  67.4 8.9 copy.264
  76.4 16.0 %pad_maximum_fusion = f32[4,19,16,16,18]{4,3,2,0,1:T(8,128)} fusion(f32[4,19,16,16,1]{4,3,2,0,1:T(8,128)} %copy.264, f32[4,19,16,16,16]{4,3,2,0,1:T(8,128)} %reshape.474, f32[4,19,16,16,1]{4,3,2,0,1:T(8,128)} %copy.263), kind=kLoop, calls=%fused_computation.72 | loop fusion | flops 700416 | bytes 2801664 | tf_op jit(solution)/shard_map/concatenate | solution.py:168
  92.3 4.5 gather_fusion.10
  98.5 4.6 gather_fusion.8
  115.5 4.6 gather_fusion.6
  121.2 4.6 gather_fusion.3
  126.7 5.1 copy.324
  131.8 6.6 pad.43.clone
  138.4 47.9 %all-gather.15.cloned.1.call-done = f32[256,5,288]{2,1,0:T(8,128)} async-done(((f32[4,5,288]{2,1,0:T(8,128)}), f32[256,5,288]{2,1,0:T(8,128)}) %all-gather.15.cloned.1.call-update) | async-done | bytes 1474576 | tf_op jit(solution)/shard_map/all_gather | solution.py:256
  189.0 82.1 %all-gather.13.cloned.1.call-done = f32[256,5,288]{2,1,0:T(8,128)} async-done(((f32[4,5,288]{2,1,0:T(8,128)}), f32[256,5,288]{2,1,0:T(8,128)}) %all-gather.13.cloned.1.call-update) | async-done | bytes 1474576 | tf_op jit(solution)/shard_map/all_gather | solution.py:255
  273.7 82.1 %all-gather.11.cloned.1.call-done = f32[256,5,288]{2,1,0:T(8,128)} async-done(((f32[4,5,288]{2,1,0:T(8,128)}), f32[256,5,288]{2,1,0:T(8,128)}) %all-gather.11.cloned.1.call-update) | async-done | bytes 1474576 | tf_op jit(solution)/shard_map/all_gather | solution.py:254
  363.8 76.6 %all-gather.9.cloned.1.call-done = f32[256,5,288]{2,1,0:T(8,128)} async-done(((f32[4,5,288]{2,1,0:T(8,128)}), f32[256,5,288]{2,1,0:T(8,128)}) %all-gather.9.cloned.1.call-update) | async-done | bytes 1474576 | tf_op jit(solution)/shard_map/all_gather | solution.py:253
  448.5 49.7 %while.16 = (s32[]{:T(128)}, f32[4,19,18,18,18]{4,3,0,2,1:T(8,128)}, s32[5,3]{0,1:T(4,128)S(1)}, f32[5,4,16,18]{3,2,1,0:T(8,128)S(1)}, s32[]{:T(128)}, /*index=5*/s32[5]{0:T(128)S(1)}, s32[1]{0:T(128)}, s32[]{:T(128)}) while((s32[]{:T(128)}, f32[4,19,18,18,18]{4,3,0,2,1:T(8,128)}, s32[5,3]{0,1:T(4,128)S(1)}, f32[5,4,16,18]{3,2,1,0:T(8,128)S(1)}, ...), condition=%wide.while_cond.8, body=%wide.while_body.8.sunk | while | flops 1173 | bytes 23287 | solution.py:208
  498.1 50.1 %while.17 = (s32[]{:T(128)}, f32[4,19,18,18,18]{4,3,0,2,1:T(8,128)}, s32[5,3]{0,1:T(4,128)S(1)}, f32[5,4,16,18]{3,2,1,0:T(8,128)S(1)}, s32[]{:T(128)}, /*index=5*/s32[5]{0:T(128)S(1)}, s32[1]{0:T(128)}, s32[]{:T(128)}) while((s32[]{:T(128)}, f32[4,19,18,18,18]{4,3,0,2,1:T(8,128)}, s32[5,3]{0,1:T(4,128)S(1)}, f32[5,4,16,18]{3,2,1,0:T(8,128)S(1)}, ...), condition=%wide.while_cond.9, body=%wide.while_body.9.sunk | while | flops 1173 | bytes 23287 | solution.py:209
  504.8 3.4 dynamic-update-slice.197
  514.8 3.4 dynamic-update-slice.197
  548.2 14.3 copy.273
  562.5 49.9 %while.18 = (s32[]{:T(128)}, f32[4,19,18,18,18]{4,2,0,3,1:T(8,128)}, s32[5,3]{0,1:T(4,128)S(1)}, f32[5,4,16,18]{3,2,1,0:T(8,128)S(1)}, s32[]{:T(128)}, /*index=5*/s32[5]{0:T(128)S(1)}, s32[1]{0:T(128)}, s32[]{:T(128)}) while((s32[]{:T(128)}, f32[4,19,18,18,18]{4,2,0,3,1:T(8,128)}, s32[5,3]{0,1:T(4,128)S(1)}, f32[5,4,16,18]{3,2,1,0:T(8,128)S(1)}, ...), condition=%wide.while_cond.10, body=%wide.while_body.10.sunk | while | flops 1173 | bytes 23287 | solution.py:210
  565.8 3.3 bitcast_select_fusion.18
  605.7 3.3 bitcast_select_fusion.18
  612.4 49.9 %while.19 = (s32[]{:T(128)}, f32[4,19,18,18,18]{4,2,0,3,1:T(8,128)}, s32[5,3]{0,1:T(4,128)S(1)}, f32[5,4,16,18]{3,2,1,0:T(8,128)S(1)}, s32[]{:T(128)}, /*index=5*/s32[5]{0:T(128)S(1)}, s32[1]{0:T(128)}, s32[]{:T(128)}) while((s32[]{:T(128)}, f32[4,19,18,18,18]{4,2,0,3,1:T(8,128)}, s32[5,3]{0,1:T(4,128)S(1)}, f32[5,4,16,18]{3,2,1,0:T(8,128)S(1)}, ...), condition=%wide.while_cond.11, body=%wide.while_body.11.sunk | while | flops 1173 | bytes 23287 | solution.py:211
  615.7 3.3 bitcast_select_fusion.19
  625.7 3.3 bitcast_select_fusion.19
  635.7 3.3 bitcast_select_fusion.19
  662.3 14.1 copy.280
  706.0 3.8 copy-done.2
  709.8 7.9 reshape.489
  723.6 3.5 fusion.3
  728.0 7.5 reshape.490
  735.4 4.5 gather_fusion.22
  740.0 6.0 gather_fusion.21
  753.3 3.4 collective-permute-start.3
  757.7 8.9 copy.303
  767.5 8.9 copy.304
  776.4 16.0 %pad_maximum_fusion.1 = f32[4,19,16,16,18]{4,3,2,0,1:T(8,128)} fusion(f32[4,19,16,16,1]{4,3,2,0,1:T(8,128)} %copy.304, f32[4,19,16,16,16]{4,3,2,0,1:T(8,128)} %reshape.490, f32[4,19,16,16,1]{4,3,2,0,1:T(8,128)} %copy.303), kind=kLoop, calls=%fused_computation.73 | loop fusion | flops 700416 | bytes 2801664 | tf_op jit(solution)/shard_map/concatenate | solution.py:168
  792.4 4.5 gather_fusion.26
  798.2 4.5 gather_fusion.25
  804.1 4.5 gather_fusion.24
  809.7 4.6 gather_fusion.23
  815.2 5.1 copy.325
  820.3 6.6 pad.44.clone
  827.0 53.3 %all-gather.23.cloned.1.call-done = f32[256,5,288]{2,1,0:T(8,128)} async-done(((f32[4,5,288]{2,1,0:T(8,128)}), f32[256,5,288]{2,1,0:T(8,128)}) %all-gather.23.cloned.1.call-update) | async-done | bytes 1474576 | tf_op jit(solution)/shard_map/all_gather | solution.py:256
  882.9 81.9 %all-gather.21.cloned.1.call-done = f32[256,5,288]{2,1,0:T(8,128)} async-done(((f32[4,5,288]{2,1,0:T(8,128)}), f32[256,5,288]{2,1,0:T(8,128)}) %all-gather.21.cloned.1.call-update) | async-done | bytes 1474576 | tf_op jit(solution)/shard_map/all_gather | solution.py:255
  967.5 82.1 %all-gather.19.cloned.1.call-done = f32[256,5,288]{2,1,0:T(8,128)} async-done(((f32[4,5,288]{2,1,0:T(8,128)}), f32[256,5,288]{2,1,0:T(8,128)}) %all-gather.19.cloned.1.call-update) | async-done | bytes 1474576 | tf_op jit(solution)/shard_map/all_gather | solution.py:254
  1057.7 76.7 %all-gather.17.cloned.1.call-done = f32[256,5,288]{2,1,0:T(8,128)} async-done(((f32[4,5,288]{2,1,0:T(8,128)}), f32[256,5,288]{2,1,0:T(8,128)}) %all-gather.17.cloned.1.call-update) | async-done | bytes 1474576 | tf_op jit(solution)/shard_map/all_gather | solution.py:253
  1142.4 49.7 %while.20 = (s32[]{:T(128)}, f32[4,19,18,18,18]{4,3,0,2,1:T(8,128)}, s32[5,3]{0,1:T(4,128)S(1)}, f32[5,4,16,18]{3,2,1,0:T(8,128)S(1)}, s32[]{:T(128)}, /*index=5*/s32[5]{0:T(128)S(1)}, s32[1]{0:T(128)}, s32[]{:T(128)}) while((s32[]{:T(128)}, f32[4,19,18,18,18]{4,3,0,2,1:T(8,128)}, s32[5,3]{0,1:T(4,128)S(1)}, f32[5,4,16,18]{3,2,1,0:T(8,128)S(1)}, ...), condition=%wide.while_cond.12, body=%wide.while_body.12.sunk | while | flops 1173 | bytes 23287 | solution.py:208
  1192.1 50.1 %while.21 = (s32[]{:T(128)}, f32[4,19,18,18,18]{4,3,0,2,1:T(8,128)}, s32[5,3]{0,1:T(4,128)S(1)}, f32[5,4,16,18]{3,2,1,0:T(8,128)S(1)}, s32[]{:T(128)}, /*index=5*/s32[5]{0:T(128)S(1)}, s32[1]{0:T(128)}, s32[]{:T(128)}) while((s32[]{:T(128)}, f32[4,19,18,18,18]{4,3,0,2,1:T(8,128)}, s32[5,3]{0,1:T(4,128)S(1)}, f32[5,4,16,18]{3,2,1,0:T(8,128)S(1)}, ...), condition=%wide.while_cond.13, body=%wide.while_body.13.sunk | while | flops 1173 | bytes 23287 | solution.py:209
  1198.7 3.4 dynamic-update-slice.201
  1208.8 3.4 dynamic-update-slice.201
  1242.2 14.2 copy.312
  1256.4 49.9 %while.22 = (s32[]{:T(128)}, f32[4,19,18,18,18]{4,2,0,3,1:T(8,128)}, s32[5,3]{0,1:T(4,128)S(1)}, f32[5,4,16,18]{3,2,1,0:T(8,128)S(1)}, s32[]{:T(128)}, /*index=5*/s32[5]{0:T(128)S(1)}, s32[1]{0:T(128)}, s32[]{:T(128)}) while((s32[]{:T(128)}, f32[4,19,18,18,18]{4,2,0,3,1:T(8,128)}, s32[5,3]{0,1:T(4,128)S(1)}, f32[5,4,16,18]{3,2,1,0:T(8,128)S(1)}, ...), condition=%wide.while_cond.14, body=%wide.while_body.14.sunk | while | flops 1173 | bytes 23287 | solution.py:210
  1279.7 3.3 bitcast_select_fusion.22
  1289.7 3.3 bitcast_select_fusion.22
  1306.3 49.9 %while.23 = (s32[]{:T(128)}, f32[4,19,18,18,18]{4,2,0,3,1:T(8,128)}, s32[5,3]{0,1:T(4,128)S(1)}, f32[5,4,16,18]{3,2,1,0:T(8,128)S(1)}, s32[]{:T(128)}, /*index=5*/s32[5]{0:T(128)S(1)}, s32[1]{0:T(128)}, s32[]{:T(128)}) while((s32[]{:T(128)}, f32[4,19,18,18,18]{4,2,0,3,1:T(8,128)}, s32[5,3]{0,1:T(4,128)S(1)}, f32[5,4,16,18]{3,2,1,0:T(8,128)S(1)}, ...), condition=%wide.while_cond.15, body=%wide.while_body.15.sunk | while | flops 1173 | bytes 23287 | solution.py:211
  1339.5 3.3 bitcast_select_fusion.23
  1356.1 14.1 copy.316
  1415.1 7.7 reshape.505
  (561 shorter events, 533.8 us)
Async XLA Ops:
  6.5 3.7 copy-start.11
  6.5 3.7 copy-start.7
  6.5 3.7 copy-start.1
  6.5 179.7 %all-gather.15.cloned.1.call-start = ((), (), s32[]{:S(2)}) async-start(), calls=%async_computation.3 | async-start | bytes 3194880 | tf_op jit(solution)/shard_map/all_gather | solution.py:256
  15.8 4.4 copy-start.8
  25.9 7.5 copy-start.9
  25.9 7.4 copy-start.10
  38.8 27.6 %collective-permute-start.1 = (f32[4,5,256]{2,0,1:T(4,128)S(1)}, f32[4,5,256]{2,0,1:T(4,128)S(1)}, u32[]{:S(2)}, u32[]{:S(2)}) collective-permute-start(f32[4,5,256]{2,0,1:T(4,128)S(1)} %reshape_squeeze.37), channel_id=1, source_target_pairs={{64,0},{128,64},{192,128},{256,192},{320,256},{384,320},{448,384},... | collective-permute-start | bytes 61448 | tf_op jit(solution)/shard_map/ppermute | solution.py:66
  49.3 3.5 copy-start.16
  49.3 3.5 copy-start.17
  50.9 5.7 collective-permute-start
  98.1 173.0 %all-gather.13.cloned.1.call-start = ((), (), s32[]{:S(2)}) async-start(), calls=%async_computation.2 | async-start | bytes 3194880 | tf_op jit(solution)/shard_map/all_gather | solution.py:255
  98.5 5.9 copy-start
  98.5 6.0 copy-start.12
  104.4 251.4 %all-gather.11.cloned.1.call-start = ((), (), s32[]{:S(2)}) async-start(), calls=%async_computation.1 | async-start | bytes 3194880 | tf_op jit(solution)/shard_map/all_gather | solution.py:254
  106.8 8.7 copy-start.14
  106.8 8.7 copy-start.15
  120.9 319.5 %all-gather.9.cloned.1.call-start = ((), (), s32[]{:S(2)}) async-start(), calls=%async_computation | async-start | bytes 3194880 | tf_op jit(solution)/shard_map/all_gather | solution.py:253
  126.6 753.7 %all-gather.23.cloned.1.call-start = ((), (), s32[]{:S(2)}) async-start(), calls=%async_computation.7 | async-start | bytes 3194880 | tf_op jit(solution)/shard_map/all_gather | solution.py:256
  138.4 310.0 %copy-start.6 = (s32[5,3]{0,1:T(4,128)S(1)}, s32[5,3]{0,1:T(4,128)}, u32[]{:S(2)}) copy-start(s32[5,3]{0,1:T(4,128)} %constant.479) | copy-start | bytes 184
  138.4 310.0 %copy-start.19 = (s32[5]{0:T(128)S(1)}, s32[5]{0:T(128)}, u32[]{:S(2)}) copy-start(s32[5]{0:T(128)} %constant.1068) | copy-start | bytes 64
  138.4 359.7 %copy-start.5 = (s32[5,3]{0,1:T(4,128)S(1)}, s32[5,3]{0,1:T(4,128)}, u32[]{:S(2)}) copy-start(s32[5,3]{0,1:T(4,128)} %constant.481) | copy-start | bytes 184
  548.2 14.3 copy-start.4
  548.2 14.3 copy-start.18
  548.2 64.2 %copy-start.3 = (s32[5,3]{0,1:T(4,128)S(1)}, s32[5,3]{0,1:T(4,128)}, u32[]{:S(2)}) copy-start(s32[5,3]{0,1:T(4,128)} %constant.485) | copy-start | bytes 184
  706.0 3.8 copy-start.2
  749.3 7.4 collective-permute-start.2
  753.3 13.2 collective-permute-start.3
  798.1 166.7 %all-gather.21.cloned.1.call-start = ((), (), s32[]{:S(2)}) async-start(), calls=%async_computation.6 | async-start | bytes 3194880 | tf_op jit(solution)/shard_map/all_gather | solution.py:255
  804.0 245.6 %all-gather.19.cloned.1.call-start = ((), (), s32[]{:S(2)}) async-start(), calls=%async_computation.5 | async-start | bytes 3194880 | tf_op jit(solution)/shard_map/all_gather | solution.py:254
  809.4 324.9 %all-gather.17.cloned.1.call-start = ((), (), s32[]{:S(2)}) async-start(), calls=%async_computation.4 | async-start | bytes 3194880 | tf_op jit(solution)/shard_map/all_gather | solution.py:253
  1415.1 7.7 copy-start.13
Sparse Core Ops, SparseCore 0:
  98.2 88.0 all-gather.14
  189.6 81.3 all-gather.12
  274.4 81.3 all-gather.10
  359.0 81.3 all-gather.8
  798.3 81.9 all-gather.22
  883.4 81.3 all-gather.20
  968.2 81.3 all-gather.18
  1052.9 81.3 all-gather.16
where the time goes:
time: 1450 us; the launch traced here: 1430 us
  local copies, waits for them, and re-layouts  598 us (41%)
  waiting for transfers between devices  586 us (40%)
  other arithmetic  203 us (14%)
  starting transfers between devices  15.3 us (1%)
  between operations  15.3 us (1%)
    scatter x160, local copies, waits for them, and re-layouts  239 us
    all_gather x2, waiting for transfers between devices, shards(): lax.all_gather(xminus, 'plane', axis=0, tiled=True)  164 us
    all_gather x2, waiting for transfers between devices, shards(): lax.all_gather(yplus, 'plane', axis=0, tiled=True)  164 us
    scatter x80, other arithmetic  160 us
    all_gather x2, waiting for transfers between devices, shards(): lax.all_gather(xplus, 'plane', axis=0, tiled=True)  153 us
    unnamed x91, local copies, waits for them, and re-layouts  103 us
    all_gather x2, waiting for transfers between devices, shards(): lax.all_gather(yminus, 'plane', axis=0, tiled=True)  101 us
    gather x16, local copies, waits for them, and re-layouts, shards(): jnp.take(tables[table_order[which]], sources[which], axis=0)  39 us
  transfers between devices with their start and end apart: 12, of which 9 were waited for; matrix products, arithmetic and copies ran while one was open for 8% of the time, Pallas kernels for 0%

commit v1 on v0

v1 whole, which is shorter than its diff:
```python
import functools

import jax
import jax.numpy as jnp
from jax import lax
from jax.experimental import pallas as pl
from jax.experimental.pallas import tpu as pltpu
from jax.sharding import PartitionSpec as P

MESH = pl.DeviceIdType.MESH
BE = 16
CAP = 4
STEPS = 2
Q = 19
F32 = jnp.float32
PLANE_DIMS = {64: (4, 8, 2)}

DIRS = [
    (0, 0, 0),
    (1, 0, 0),
    (-1, 0, 0),
    (0, 1, 0),
    (0, -1, 0),
    (0, 0, 1),
    (0, 0, -1),
    (1, 1, 0),
    (-1, -1, 0),
    (1, -1, 0),
    (-1, 1, 0),
    (1, 0, 1),
    (-1, 0, -1),
    (1, 0, -1),
    (-1, 0, 1),
    (0, 1, 1),
    (0, -1, -1),
    (0, 1, -1),
    (0, -1, 1),
]
OPP = [0, 2, 1, 4, 3, 6, 5, 8, 7, 10, 9, 12, 11, 14, 13, 16, 15, 18, 17]
WEIGHTS = [1.0 / 3.0] + [1.0 / 18.0] * 6 + [1.0 / 36.0] * 12
ZPLUS = [5, 11, 14, 15, 18]
ZMINUS = [6, 12, 13, 16, 17]
OFF = [1 if d[1] > 0 else 0 for d in DIRS]
HALO = [0 if d[1] > 0 else 2 for d in DIRS]
MAIN = slice(8, 24)
LOW, HIGH = slice(7, 8), slice(24, 25)
FIRST, LAST = slice(8, 9), slice(23, 24)


def sources_kernel(slots_ref, near_ref, out_ref):
    blocks, slots = near_ref.shape[0], slots_ref.shape[1]
    held = slots_ref[...]
    onehot = lax.broadcasted_iota(jnp.int32, (blocks, slots), 0) == held
    number = lax.broadcasted_iota(jnp.int32, (blocks, slots), 1).astype(F32)
    lookup = jnp.sum(jnp.where(onehot, number, 0.0), axis=1, keepdims=True)
    lane = lax.broadcasted_iota(jnp.int32, (blocks, blocks), 1)
    hops = [(near_ref[:, k : k + 1] == lane).astype(F32) for k in range(4)]

    def through(k, column):
        wide = jnp.broadcast_to(column, (blocks, 128))
        return jnp.dot(
            hops[k], wide, preferred_element_type=F32, precision=lax.Precision.HIGHEST
        )[:, :1]

    one = [through(k, lookup) for k in range(4)]
    two = [through(0, one[2]), through(1, one[3]), through(0, one[3]), through(1, one[2])]
    place = lax.broadcasted_iota(jnp.int32, (blocks, 8), 1)
    table = jnp.zeros((blocks, 8), F32)
    for k, column in enumerate(one + two):
        table = jnp.where(place == k, column, table)
    found = lax.dot_general(
        table,
        onehot.astype(F32),
        (((0,), (0,)), ((), ())),
        preferred_element_type=F32,
        precision=lax.Precision.HIGHEST,
    )
    out_ref[0:8, :] = (found + 0.5).astype(jnp.int32)
    out_ref[8:16, :] = jnp.broadcast_to((held < blocks).astype(jnp.int32), (8, slots))


def collided(f, fluid):
    s1, d1 = f[1] + f[2], f[1] - f[2]
    s2, d2 = f[3] + f[4], f[3] - f[4]
    s3, d3 = f[5] + f[6], f[5] - f[6]
    a, da = f[7] + f[8], f[7] - f[8]
    b, db = f[9] + f[10], f[9] - f[10]
    c, dc = f[11] + f[12], f[11] - f[12]
    d, dd = f[13] + f[14], f[13] - f[14]
    e, de = f[15] + f[16], f[15] - f[16]
    g, dg = f[17] + f[18], f[17] - f[18]
    sxy, sxz, syz = a + b, c + d, e + g
    x_xy, y_xy = da + db, da - db
    x_xz, z_xz = dc + dd, dc - dd
    y_yz, z_yz = de + dg, de - dg
    axis = s1 + s2 + s3
    diag = sxy + sxz + syz
    xx, yy, zz = x_xy + x_xz, y_xy + y_yz, z_xz + z_yz
    rho = f[0] + axis + diag
    jx, jy, jz = d1 + xx, d2 + yy, d3 + zz
    jx2, jy2, jz2 = jx * jx, jy * jy, jz * jz
    jsq = jx2 + jy2 + jz2
    pxx_eq = 2.0 * jx2 - jy2 - jz2
    pww_eq = jy2 - jz2
    m_e = 8.0 * diag - 11.0 * axis - 30.0 * f[0]
    m_eps = diag - 4.0 * axis + 12.0 * f[0]
    yz_axis = s2 + s3
    part = sxy + sxz - 2.0 * syz
    split = sxy - sxz
    turn = s2 - s3
    k_e = (1.19 / 2394.0) * (m_e + 11.0 * rho - 19.0 * jsq)
    k_eps = (1.4 / 252.0) * (m_eps - 3.0 * rho + 5.5 * jsq)
    k_qx = (1.2 / 40.0) * (xx - 4.0 * d1 + (2.0 / 3.0) * jx)
    k_qy = (1.2 / 40.0) * (yy - 4.0 * d2 + (2.0 / 3.0) * jy)
    k_qz = (1.2 / 40.0) * (zz - 4.0 * d3 + (2.0 / 3.0) * jz)
    k_pxx = (1.25 / 36.0) * (2.0 * s1 - yz_axis + part - pxx_eq)
    k_pixx = (1.4 / 72.0) * (2.0 * yz_axis - 4.0 * s1 + part + 0.5 * pxx_eq)
    k_pww = (1.25 / 12.0) * (turn + split - pww_eq)
    k_piww = (1.4 / 24.0) * (split - 2.0 * turn + 0.5 * pww_eq)
    k_pxy = (1.25 / 4.0) * (a - b - jx * jy)
    k_pyz = (1.25 / 4.0) * (e - g - jy * jz)
    k_pxz = (1.25 / 4.0) * (c - d - jx * jz)
    k_mx = (1.98 / 8.0) * (x_xy - x_xz)
    k_my = (1.98 / 8.0) * (y_yz - y_xy)
    k_mz = (1.98 / 8.0) * (z_xz - z_yz)
    axial = 11.0 * k_e + 4.0 * k_eps
    sides = k_pxx - 2.0 * k_pixx
    tilt = k_pww - 2.0 * k_piww
    ax = 2.0 * sides - axial
    ay = tilt - sides - axial
    az = -tilt - sides - axial
    even = 8.0 * k_e + k_eps
    both = k_pxx + k_pixx
    lean = k_pww + k_piww
    exy = even + both + lean
    exz = even + both - lean
    eyz = even - 2.0 * both
    ux, uy, uz = 4.0 * k_qx, 4.0 * k_qy, 4.0 * k_qz
    xy_x, xy_y = k_qx + k_mx, k_qy - k_my
    xz_x, xz_z = k_qx - k_mx, k_qz + k_mz
    yz_y, yz_z = k_qy + k_my, k_qz - k_mz
    p, m = exy + k_pxy, exy - k_pxy
    add, sub = xy_x + xy_y, xy_x - xy_y
    change = [12.0 * k_eps - 30.0 * k_e, ax - ux, ax + ux, ay - uy, ay + uy, az - uz, az + uz]
    change += [p + add, p - add, m + sub, m - sub]
    p, m = exz + k_pxz, exz - k_pxz
    add, sub = xz_x + xz_z, xz_x - xz_z
    change += [p + add, p - add, m + sub, m - sub]
    p, m = eyz + k_pyz, eyz - k_pyz
    add, sub = yz_y + yz_z, yz_y - yz_z
    change += [p + add, p - add, m + sub, m - sub]
    return [jnp.where(fluid, f[i] - change[i], f[OPP[i]]) for i in range(Q)]


def skewed(rows, base, stride):
    return pltpu.roll(rows, base, 1, stride=stride, stride_axis=0)


def spread(rows, turns):
    for t in turns:
        rows = rows + pltpu.roll(rows, t, 1)
    return rows


def kernel(dims, near_ref, pop_ref, mask_ref, out_ref, tiles, field, fluid, ext, *rest):
    nx, nz, nc = dims
    nd = lax.axis_size("depth")
    per_x = nz * nc * CAP
    layer = lax.axis_index("depth")
    me = lax.axis_index("plane")
    core = me % nc
    z = (me // nc) % nz
    x = me // (nc * nz)
    turn = 1 - 2 * core
    mine = (z * nc + core) * CAP
    first_slot = me * CAP

    def plane(xx, zz, cc):
        return {"plane": (xx * nz + zz) * nc + cc}

    above = {"depth": (layer + 1) % nd}
    below = {"depth": (layer + nd - 1) % nd}
    ring_a = plane(x, (z + turn + nz) % nz, core)
    ring_b = plane(x, (z - turn + nz) % nz, core)
    twin = plane(x, z, 1 - core)
    across = [plane((x + k) % nx, z, core) for k in range(1, nx)]

    barrier = pltpu.get_barrier_semaphore()
    partners = [above, below, ring_a, ring_b, twin] + across
    for other in partners:
        pl.semaphore_signal(barrier, inc=1, device_id=other, device_id_type=MESH)

    send_sems, recv_sems = rest[-2:]
    per_step = rest[:-2]
    used = [0]

    def copy(src, dst, device):
        n = used[0]
        used[0] += 1
        return pltpu.make_async_remote_copy(
            src_ref=src,
            dst_ref=dst,
            send_sem=send_sems.at[n],
            recv_sem=recv_sems.at[n],
            device_id=device,
            device_id_type=MESH,
        )

    lane = lax.broadcasted_iota(jnp.int32, (BE, 128), 1)
    row = lax.broadcasted_iota(jnp.int32, (BE, 128), 0)
    zin = lane % BE
    low_lanes, high_lanes = lane < BE, lane >= 128 - BE
    own_row = zin == row
    own_group = lane // BE == row % 8
    tile_row = lax.broadcasted_iota(jnp.int32, (8, 128), 0)

    for t in range(32):
        tiles[0, 8 * t : 8 * t + CAP, :] = mask_ref[0, :, 128 * t : 128 * t + 128].astype(F32)
    for s in range(CAP):
        for h in range(2):
            fluid[s, h] = tiles[0, pl.ds(8 * h + s, BE, stride=16), :]

    def take_in(s, carry):
        for g in range(3):
            rows = min(8, Q - 8 * g)
            for t in range(32):
                tiles[g, 8 * t : 8 * t + rows, :] = pop_ref[
                    0, s, 8 * g : 8 * g + rows, 128 * t : 128 * t + 128
                ]
        for i in range(Q):
            for h in range(2):
                part = tiles[i // 8, pl.ds(8 * h + i % 8, BE, stride=16), :]
                field[s, i, h] = part * WEIGHTS[i]
        return carry

    lax.fori_loop(0, CAP, take_in, 0)

    def collide_all(up, down):
        def body(n, carry):
            s, h = n // 2, n % 2
            f = [field[s, i, h] for i in range(Q)]
            post = collided(f, fluid[s, h] == 1.0)
            for i in range(Q):
                ext[s, i, h + OFF[i], MAIN, :] = post[i]
            for k, i in enumerate(ZPLUS):
                packed = jnp.where(own_row, skewed(post[i], 1, 1), 0.0)
                up[pl.ds(s * 10 + k * 2 + h, 1), :] = jnp.sum(packed, axis=0, keepdims=True)
            for k, i in enumerate(ZMINUS):
                packed = jnp.where(own_row, skewed(post[i], 0, 1), 0.0)
                down[pl.ds(s * 10 + k * 2 + h, 1), :] = jnp.sum(packed, axis=0, keepdims=True)
            return carry

        lax.fori_loop(0, 2 * CAP, body, 0)

    def put_y(table, s, tile, start, i):
        if DIRS[i][1] > 0:
            moved = skewed(ext[s, i, 2, MAIN, :], BE, BE)
        else:
            moved = skewed(ext[s, i, 0, MAIN, :], 0, BE)
        kept = jnp.where(own_group, moved, 0.0)
        for q in range(2):
            table[mine + s, tile, start + q : start + q + 1, :] = jnp.sum(
                kept[8 * q : 8 * q + 8], axis=0, keepdims=True
            )

    def put_x(table, s, tile, start, i):
        edge = LAST if DIRS[i][0] > 0 else FIRST
        for h in range(2):
            table[mine + s, tile, start + h : start + h + 1, :] = ext[s, i, h + OFF[i], edge, :]

    def pack_early(table):
        def body(s, carry):
            for k, i in enumerate((1, 7, 9)):
                put_x(table, s, 0, 2 * k, i)
            table[mine + s, 0, 6:7, :] = ext[s, 7, 2, LAST, :]
            table[mine + s, 0, 7:8, :] = ext[s, 9, 0, LAST, :]
            for k, i in enumerate((2, 8, 10)):
                put_x(table, s, 1, 2 * k, i)
            table[mine + s, 1, 6:7, :] = ext[s, 8, 0, FIRST, :]
            table[mine + s, 1, 7:8, :] = ext[s, 10, 2, FIRST, :]
            for k, i in enumerate((3, 7, 10)):
                put_y(table, s, 2, 2 * k, i)
                put_y(table, s, 3, 2 * k, OPP[i])
            for tile in (2, 3):
                table[mine + s, tile, 6:8, :] = jnp.zeros((2, 128), F32)
            return carry

        lax.fori_loop(0, CAP, body, 0)

    def shift_z(from_below, from_above, table):
        def body(s, carry):
            for k, i in enumerate(ZPLUS):
                for h in range(2):
                    rim = from_below[pl.ds(s * 10 + k * 2 + h, 1), :]
                    rim = jnp.broadcast_to(pltpu.roll(rim, 128 - BE, 1), (BE, 128))
                    rim = spread(jnp.where(own_row, rim, 0.0), (120, 124, 126, 127))
                    part = ext[s, i, h + OFF[i], MAIN, :]
                    ext[s, i, h + OFF[i], MAIN, :] = jnp.where(
                        zin == 0, rim, pltpu.roll(part, 1, 1)
                    )
            for k, i in enumerate(ZMINUS):
                for h in range(2):
                    rim = from_above[pl.ds(s * 10 + k * 2 + h, 1), :]
                    rim = jnp.broadcast_to(rim, (BE, 128))
                    rim = spread(jnp.where(own_row, rim, 0.0), (8, 4, 2, 1))
                    part = ext[s, i, h + OFF[i], MAIN, :]
                    ext[s, i, h + OFF[i], MAIN, :] = jnp.where(
                        zin == BE - 1, rim, pltpu.roll(part, 127, 1)
                    )
            for k, i in enumerate((11, 13, 12, 14)):
                put_x(table, s, 0, 2 * k, i)
            for k, i in enumerate((15, 17, 16, 18)):
                put_y(table, s, 1, 2 * k, i)
            return carry

        lax.fori_loop(0, CAP, body, 0)

    class Ring:
        def __init__(self, table):
            def block(zz):
                return table.at[pl.ds((((zz + 2 * nz) % nz) * nc + core) * CAP, CAP)]

            self.a = [
                copy(block(z - turn * t), block(z - turn * t), ring_a) for t in range(nz // 2)
            ]
            self.b = [
                copy(block(z + turn * t), block(z + turn * t), ring_b)
                for t in range((nz - 1) // 2)
            ]
            self.twin = [copy(block(z), block(z), twin)]
            self.twin += [
                copy(block(z - turn * t), block(z - turn * t), twin)
                for t in range(1, nz // 2 + 1)
            ]
            self.twin_b = len(self.twin)
            self.twin += [
                copy(block(z + turn * t), block(z + turn * t), twin)
                for t in range(1, (nz - 1) // 2 + 1)
            ]

        def begin(self):
            self.a[0].start()
            if self.b:
                self.b[0].start()
            self.twin[0].start()

        def hop(self, t):
            if t <= len(self.a):
                self.a[t - 1].wait_recv()
                if t < len(self.a):
                    self.a[t].start()
                self.twin[t].start()
            if t <= len(self.b):
                self.b[t - 1].wait_recv()
                if t < len(self.b):
                    self.b[t].start()
                self.twin[self.twin_b + t - 1].start()

        def end(self):
            for c in self.twin:
                c.wait_recv()

        def sent(self):
            for c in self.a + self.b + self.twin:
                c.wait_send()

    def source(k, xx, s):
        return near_ref[k, xx * per_x + mine + s]

    def early_row(table, to, base, xx):
        def body(s, carry):
            at = [source(k, xx, s) % per_x for k in range(8)]
            for tile, (main, six, seven) in enumerate(((0, 4, 6), (1, 5, 7))):
                got = jnp.where(tile_row == 6, table[at[six], tile], table[at[main], tile])
                to[base + s, tile] = jnp.where(tile_row == 7, table[at[seven], tile], got)
            to[base + s, 2] = table[at[2], 2]
            to[base + s, 3] = table[at[3], 3]
            return carry

        lax.fori_loop(0, CAP, body, 0)

    def late_row(table, to, base, xx):
        def body(s, carry):
            at = [source(k, xx, s) % per_x for k in range(4)]
            for tile in range(2):
                to[base + s, tile] = jnp.where(
                    tile_row < 4, table[at[2 * tile], tile], table[at[2 * tile + 1], tile]
                )
            return carry

        lax.fori_loop(0, CAP, body, 0)

    def hand_out(fill, table, out, got):
        sends = []
        for k in range(1, nx):
            fill(table, out, (k - 1) * CAP, (x + k) % nx)
            c = copy(
                out.at[pl.ds((k - 1) * CAP, CAP)], got.at[pl.ds(x * CAP, CAP)], across[k - 1]
            )
            c.start()
            sends.append(c)
        fill(table, got, x * CAP, x)
        return sends

    def take_y(s, i, two):
        wide = [jnp.broadcast_to(two[q : q + 1], (8, 128)) for q in range(2)]
        kept = jnp.where(own_group, jnp.concatenate(wide, axis=0), 0.0)
        ext[s, i, HALO[i], MAIN, :] = spread(kept, (64, 32, 16))

    def place_halos(early, late):
        def body(s, carry):
            of = [(source(k, x, s) // per_x) * CAP + s for k in range(8)]

            def put(i, h, value):
                ext[s, i, h, LOW if DIRS[i][0] > 0 else HIGH, :] = value

            for tile, faces in enumerate(((1, 7, 9), (2, 8, 10))):
                for k, i in enumerate(faces):
                    for h in range(2):
                        r = 2 * k + h
                        put(i, h + OFF[i], early[of[tile], tile, r : r + 1, :])
            put(7, 0, early[of[4], 0, 6:7, :])
            put(9, 2, early[of[6], 0, 7:8, :])
            put(8, 2, early[of[5], 1, 6:7, :])
            put(10, 0, early[of[7], 1, 7:8, :])
            for k, i in enumerate((3, 7, 10)):
                take_y(s, i, early[of[2], 2, 2 * k : 2 * k + 2, :])
                take_y(s, OPP[i], early[of[3], 3, 2 * k : 2 * k + 2, :])
            for k, i in enumerate((11, 13, 12, 14)):
                for h in range(2):
                    r = 2 * k + h
                    put(i, h, late[of[k // 2], 0, r : r + 1, :])
            for k, i in enumerate((15, 17, 16, 18)):
                take_y(s, i, late[of[2 + k // 2], 1, 2 * k : 2 * k + 2, :])
            return carry

        lax.fori_loop(0, CAP, body, 0)

    def shift_xy():
        def body(s, carry):
            for i in range(Q):
                cx, cy, _ = DIRS[i]
                rows = slice(8 - cx, 24 - cx)
                if cy == 0:
                    for h in range(2):
                        field[s, i, h] = ext[s, i, h, rows, :]
                    continue
                e = [ext[s, i, h, rows, :] for h in range(3)]
                for h in range(2):
                    if cy > 0:
                        field[s, i, h] = pltpu.roll(
                            jnp.where(high_lanes, e[h], e[h + 1]), BE, 1
                        )
                    else:
                        field[s, i, h] = pltpu.roll(
                            jnp.where(low_lanes, e[h + 1], e[h]), 128 - BE, 1
                        )
            return carry

        lax.fori_loop(0, CAP, body, 0)

    for step in range(STEPS):
        up, down, low, high, table_e, table_l, out_e, out_l, got_e, got_l = per_step[
            10 * step : 10 * step + 10
        ]
        collide_all(up, down)
        if step == 0:
            pl.semaphore_wait(barrier, len(partners))
        rims = [copy(up, low, above), copy(down, high, below)]
        for c in rims:
            c.start()
        pack_early(table_e)
        early = Ring(table_e)
        early.begin()
        for c in rims:
            c.wait_recv()
        shift_z(low, high, table_l)
        late = Ring(table_l)
        late.begin()
        hops = nz // 2
        early.hop(1)
        for t in range(2, hops + 1):
            early.hop(t)
            late.hop(t - 1)
        early.end()
        sends = hand_out(early_row, table_e, out_e, got_e)
        late.hop(hops)
        late.end()
        sends += hand_out(late_row, table_l, out_l, got_l)
        for c in sends:
            c.wait_recv()
        place_halos(got_e, got_l)
        shift_xy()
        early.sent()
        late.sent()
        for c in rims + sends:
            c.wait_send()

    def give_out(s, carry):
        held = near_ref[8, first_slot + s] == 1
        for i in range(Q):
            for h in range(2):
                part = jnp.where(held, field[s, i, h] * (1.0 / WEIGHTS[i]), 0.0)
                tiles[i // 8, pl.ds(8 * h + i % 8, BE, stride=16), :] = part
        for g in range(3):
            rows = min(8, Q - 8 * g)
            for t in range(32):
                out_ref[0, s, 8 * g : 8 * g + rows, 128 * t : 128 * t + 128] = tiles[
                    g, 8 * t : 8 * t + rows, :
                ]
        return carry

    lax.fori_loop(0, CAP, give_out, 0)


def solution(mesh):
    planes = mesh.shape["plane"]
    dims = PLANE_DIMS[planes]
    nx, nz, nc = dims
    group = nz * nc * CAP

    def shards(populations, fluid_mask, block_per_slot, neighbours):
        slots = block_per_slot.shape[0]
        near = pl.pallas_call(
            sources_kernel,
            out_shape=jax.ShapeDtypeStruct((16, slots), jnp.int32),
            in_specs=[pl.BlockSpec(memory_space=pltpu.VMEM)] * 2,
            out_specs=pl.BlockSpec(memory_space=pltpu.VMEM),
        )(block_per_slot.reshape(1, slots), neighbours)
        scratch = [
            pltpu.VMEM((3, 256, 128), F32),
            pltpu.VMEM((CAP, Q, 2, BE, 128), F32),
            pltpu.VMEM((CAP, 2, BE, 128), F32),
            pltpu.VMEM((CAP, Q, 3, 32, 128), F32),
        ]
        for _ in range(STEPS):
            scratch += [pltpu.VMEM((10 * CAP, 128), F32)] * 4
            for count, tiles in ((group, 4), (group, 2)):
                scratch.append(pltpu.VMEM((count, tiles, 8, 128), F32))
            for tiles in (4, 2):
                scratch.append(pltpu.VMEM(((nx - 1) * CAP, tiles, 8, 128), F32))
            for tiles in (4, 2):
                scratch.append(pltpu.VMEM((nx * CAP, tiles, 8, 128), F32))
        ring = nz // 2 + (nz - 1) // 2 + nz
        copies = STEPS * (2 + 2 * ring + 2 * (nx - 1))
        scratch += [pltpu.SemaphoreType.DMA((copies,)), pltpu.SemaphoreType.DMA((copies,))]
        vmem = pl.BlockSpec(memory_space=pltpu.VMEM)
        return pl.pallas_call(
            functools.partial(kernel, dims),
            out_shape=jax.ShapeDtypeStruct(populations.shape, F32),
            in_specs=[pl.BlockSpec(memory_space=pltpu.SMEM), vmem, vmem],
            out_specs=vmem,
            scratch_shapes=scratch,
            compiler_params=pltpu.CompilerParams(
                collective_id=0, has_side_effects=True, vmem_limit_bytes=40 * 1024 * 1024
            ),
        )(near, populations, fluid_mask)

    return jax.shard_map(
        shards,
        mesh=mesh,
        in_specs=(P("depth", "plane", None, None), P("depth", "plane", None), P(), P()),
        out_specs=P("depth", "plane", None, None),
        check_vma=False,
    )
```

time: 1450 us -> 76.6 us (0.05); the launches traced: 1430 us -> 76.4 us
  local copies, waits for them, and re-layouts: 598 us -> 5.32 us
  waiting for transfers between devices: 586 us -> 0 us
  other arithmetic: 203 us -> 0 us
  Pallas kernels: 0 us -> 71 us
  starting transfers between devices: 15.3 us -> 0 us
  between operations: 15.3 us -> 0.03 us
    all_gather x8 -> x0, waiting for transfers between devices: 583 us -> none  [the longest x2 164 us: shards(): lax.all_gather(xminus, 'plane', axis=0, tiled=True)]
    scatter x175 -> x0, local copies, waits for them, and re-layouts: 282 us -> none
    scatter x80 -> x0, other arithmetic: 160 us -> none
    gather x47 -> x0, local copies, waits for them, and re-layouts: 108 us -> none  [the longest x16 39 us: shards(): jnp.take(tables[table_order[which]], sources[which], axis=0)]
    unnamed x91 -> x6, local copies, waits for them, and re-layouts: 103 us -> 3.49 us
    pallas_call x0 -> x2, Pallas kernels: none -> 71 us  [the longest x1 68.4 us: shards(): pl.pallas_call(functools.partial(kernel, dims), out_shape=jax.ShapeDtypeS...]
    broadcast_in_dim x4 -> x0, local copies, waits for them, and re-layouts: 35.6 us -> none  [extend_depth(): return jnp.concatenate([lower[..., None], cells, upper[..., None]], axis=-1)]
    reshape x24 -> x0, local copies, waits for them, and re-layouts: 33 us -> none  [the longest x2 15.6 us: gather_layers(): return jnp.stack(pieces).reshape(19, BE * BE * BE)]
  transfers between devices with their start and end apart: 12 -> 0, of which waited for: 9 -> 0; matrix products, arithmetic and copies ran while one was open for 8% -> 0% of each run, Pallas kernels for 0% -> 0%
where the time goes in v1:
time: 76.6 us; the launch traced here: 76.4 us
  Pallas kernels  71 us (93%)
  local copies, waits for them, and re-layouts  5.32 us (7%)
    pallas_call x1, Pallas kernels, shards(): pl.pallas_call(functools.partial(kernel, dims), out_shape=jax.ShapeDtypeS...  68.4 us
    unnamed x6, local copies, waits for them, and re-layouts  3.49 us
    pallas_call x1, Pallas kernels, shards(): pl.pallas_call(sources_kernel, out_shape=jax.ShapeDtypeStruct((16, slots)...  2.63 us
    pallas_call x1, local copies, waits for them, and re-layouts, shards(): pl.pallas_call(functools.partial(kernel, dims), out_shape=jax.ShapeDtypeS...  1.84 us

profile of v1, /device:TPU:1, one launch (start us, length us, event | category | flops | bytes accessed | tf_op | source)
XLA Modules:
  0.0 76.4 jit_solution(12612239316916940237)
XLA Ops:
  0.0 0.0 copy-start.1
  0.0 1.4 %copy.5.near_ref = s32[128,4]{1,0:T(8,128)} copy(s32[128,4]{0,1:T(4,128)} %param.7) | data formatting | bytes 4096 | tf_op args[3]
  1.5 2.6 %shard_map.46.near_ref = s32[16,256]{1,0:T(8,128)} custom-call(s32[1,256]{1,0:T(1,128)} %bitcast.1, s32[128,4]{1,0:T(8,128)} %copy.5.near_ref), custom_call_target="tpu_custom_call" | custom-call | tf_op jit(solution)/shard_map/pallas_call | solution.py:524
  4.1 0.0 copy-start
  4.1 2.0 %copy.6.pop_ref = f32[1,4,19,4096]{3,2,1,0:T(8,128)S(1)} copy(f32[1,4,19,4096]{3,1,2,0:T(4,128)} %param.4) | data formatting | bytes 2490368 | tf_op args[0]
  6.1 0.0 copy-done.1
  6.1 0.0 copy-done
  6.1 68.4 %shard_map.47 = f32[1,4,19,4096]{3,2,1,0:T(8,128)S(1)} custom-call(s32[16,256]{1,0:T(8,128)S(1)} %copy-done, f32[1,4,19,4096]{3,2,1,0:T(8,128)S(1)} %copy.6.pop_ref, s32[1,4,4096]{2,1,0:T(4,128)S(1)} %copy-done.1), custom_call_target="tpu_custom_call" | custom-call | tf_op jit(solution)/shard_map/pallas_call | solution.py:548
  74.6 1.8 %copy.7 = f32[1,4,19,4096]{3,1,2,0:T(4,128)} copy(f32[1,4,19,4096]{3,2,1,0:T(8,128)S(1)} %shard_map.47) | data formatting | bytes 2490368 | tf_op jit(solution)/shard_map/pallas_call | solution.py:548
Async XLA Ops:
  0.0 6.1 %copy-start.1 = (s32[1,4,4096]{2,1,0:T(4,128)S(1)}, s32[1,4,4096]{2,1,0:T(4,128)}, u32[]{:S(2)}) copy-start(s32[1,4,4096]{2,1,0:T(4,128)} %mask_ref.1) | copy-start | bytes 196612
  4.1 2.0 %copy-start = (s32[16,256]{1,0:T(8,128)S(1)}, s32[16,256]{1,0:T(8,128)}, u32[]{:S(2)}) copy-start(s32[16,256]{1,0:T(8,128)} %shard_map.46.near_ref) | copy-start | bytes 49156

commit v2 on v1

v2 whole, which is shorter than its diff:
```python
import functools

import jax
import jax.numpy as jnp
from jax import lax
from jax.experimental import pallas as pl
from jax.experimental.pallas import tpu as pltpu
from jax.sharding import PartitionSpec as P

MESH = pl.DeviceIdType.MESH
BE = 16
CAP = 4
STEPS = 2
Q = 19
F32 = jnp.float32
PLANE_DIMS = {64: (4, 8, 2)}

DIRS = [
    (0, 0, 0),
    (1, 0, 0),
    (-1, 0, 0),
    (0, 1, 0),
    (0, -1, 0),
    (0, 0, 1),
    (0, 0, -1),
    (1, 1, 0),
    (-1, -1, 0),
    (1, -1, 0),
    (-1, 1, 0),
    (1, 0, 1),
    (-1, 0, -1),
    (1, 0, -1),
    (-1, 0, 1),
    (0, 1, 1),
    (0, -1, -1),
    (0, 1, -1),
    (0, -1, 1),
]
OPP = [0, 2, 1, 4, 3, 6, 5, 8, 7, 10, 9, 12, 11, 14, 13, 16, 15, 18, 17]
WEIGHTS = [1.0 / 3.0] + [1.0 / 18.0] * 6 + [1.0 / 36.0] * 12
ZPLUS = [5, 11, 14, 15, 18]
ZMINUS = [6, 12, 13, 16, 17]
EARLY = ((1, 7, 9), (2, 8, 10), (3, 7, 10), (4, 8, 9))
LATE = ((11, 13, 12, 14), (15, 17, 16, 18))
YDIRS = [i for i in range(Q) if DIRS[i][1] != 0]


def top_rows(v):
    total = v[0:8]
    for r in range(8, v.shape[0], 8):
        total = jnp.maximum(total, v[r : r + 8])
    for t in (4, 2, 1):
        total = jnp.maximum(total, pltpu.roll(total, t, 0))
    return total


def find_sources(slots_ref, near_ref, out_ref):
    blocks, slots = near_ref.shape[1], slots_ref.shape[1]
    held = slots_ref[...]
    down = lax.broadcasted_iota(jnp.int32, (blocks, 128), 0)
    across = lax.broadcasted_iota(jnp.int32, (blocks, 128), 1)

    def upright(line):
        return jnp.transpose(jnp.broadcast_to(line, (128, 128)))

    lookup = jnp.zeros((8, 128), jnp.int32)
    for q in range(slots // 128):
        mine = upright(held[:, 128 * q : 128 * q + 128])
        lookup = jnp.maximum(lookup, top_rows(jnp.where(mine == across, down + 128 * q, 0)))

    def through(k, column):
        hit = jnp.broadcast_to(near_ref[k : k + 1, :], (blocks, 128)) == down
        return top_rows(jnp.where(hit, column, 0))[0:1]

    column = upright(lookup[0:1])
    found = [upright(through(k, column)) for k in range(4)]
    found += [upright(through(k, found[j])) for k, j in ((0, 2), (1, 3), (0, 3), (1, 2))]
    for q in range(slots // 128):
        part = slice(128 * q, 128 * q + 128)
        hit = jnp.broadcast_to(held[:, part], (blocks, 128)) == down
        for k in range(8):
            out_ref[k : k + 1, part] = top_rows(jnp.where(hit, found[k], 0))[0:1]
        out_ref[8:16, part] = jnp.broadcast_to(
            jnp.where(held[:, part] < blocks, 1, 0), (8, 128)
        )


def collided(f, fluid):
    s1, d1 = f[1] + f[2], f[1] - f[2]
    s2, d2 = f[3] + f[4], f[3] - f[4]
    s3, d3 = f[5] + f[6], f[5] - f[6]
    a, da = f[7] + f[8], f[7] - f[8]
    b, db = f[9] + f[10], f[9] - f[10]
    c, dc = f[11] + f[12], f[11] - f[12]
    d, dd = f[13] + f[14], f[13] - f[14]
    e, de = f[15] + f[16], f[15] - f[16]
    g, dg = f[17] + f[18], f[17] - f[18]
    sxy, sxz, syz = a + b, c + d, e + g
    x_xy, y_xy = da + db, da - db
    x_xz, z_xz = dc + dd, dc - dd
    y_yz, z_yz = de + dg, de - dg
    axis = s1 + s2 + s3
    diag = sxy + sxz + syz
    xx, yy, zz = x_xy + x_xz, y_xy + y_yz, z_xz + z_yz
    rho = f[0] + axis + diag
    jx, jy, jz = d1 + xx, d2 + yy, d3 + zz
    jx2, jy2, jz2 = jx * jx, jy * jy, jz * jz
    jsq = jx2 + jy2 + jz2
    pxx_eq = 2.0 * jx2 - jy2 - jz2
    pww_eq = jy2 - jz2
    m_e = 8.0 * diag - 11.0 * axis - 30.0 * f[0]
    m_eps = diag - 4.0 * axis + 12.0 * f[0]
    yz_axis = s2 + s3
    part = sxy + sxz - 2.0 * syz
    split = sxy - sxz
    turn = s2 - s3
    k_e = (1.19 / 2394.0) * (m_e + 11.0 * rho - 19.0 * jsq)
    k_eps = (1.4 / 252.0) * (m_eps - 3.0 * rho + 5.5 * jsq)
    k_qx = (1.2 / 40.0) * (xx - 4.0 * d1 + (2.0 / 3.0) * jx)
    k_qy = (1.2 / 40.0) * (yy - 4.0 * d2 + (2.0 / 3.0) * jy)
    k_qz = (1.2 / 40.0) * (zz - 4.0 * d3 + (2.0 / 3.0) * jz)
    k_pxx = (1.25 / 36.0) * (2.0 * s1 - yz_axis + part - pxx_eq)
    k_pixx = (1.4 / 72.0) * (2.0 * yz_axis - 4.0 * s1 + part + 0.5 * pxx_eq)
    k_pww = (1.25 / 12.0) * (turn + split - pww_eq)
    k_piww = (1.4 / 24.0) * (split - 2.0 * turn + 0.5 * pww_eq)
    k_pxy = (1.25 / 4.0) * (a - b - jx * jy)
    k_pyz = (1.25 / 4.0) * (e - g - jy * jz)
    k_pxz = (1.25 / 4.0) * (c - d - jx * jz)
    k_mx = (1.98 / 8.0) * (x_xy - x_xz)
    k_my = (1.98 / 8.0) * (y_yz - y_xy)
    k_mz = (1.98 / 8.0) * (z_xz - z_yz)
    axial = 11.0 * k_e + 4.0 * k_eps
    sides = k_pxx - 2.0 * k_pixx
    tilt = k_pww - 2.0 * k_piww
    ax = 2.0 * sides - axial
    ay = tilt - sides - axial
    az = -tilt - sides - axial
    even = 8.0 * k_e + k_eps
    both = k_pxx + k_pixx
    lean = k_pww + k_piww
    exy = even + both + lean
    exz = even + both - lean
    eyz = even - 2.0 * both
    ux, uy, uz = 4.0 * k_qx, 4.0 * k_qy, 4.0 * k_qz
    xy_x, xy_y = k_qx + k_mx, k_qy - k_my
    xz_x, xz_z = k_qx - k_mx, k_qz + k_mz
    yz_y, yz_z = k_qy + k_my, k_qz - k_mz
    p, m = exy + k_pxy, exy - k_pxy
    add, sub = xy_x + xy_y, xy_x - xy_y
    change = [12.0 * k_eps - 30.0 * k_e, ax - ux, ax + ux, ay - uy, ay + uy, az - uz, az + uz]
    change += [p + add, p - add, m + sub, m - sub]
    p, m = exz + k_pxz, exz - k_pxz
    add, sub = xz_x + xz_z, xz_x - xz_z
    change += [p + add, p - add, m + sub, m - sub]
    p, m = eyz + k_pyz, eyz - k_pyz
    add, sub = yz_y + yz_z, yz_y - yz_z
    change += [p + add, p - add, m + sub, m - sub]
    return [jnp.where(fluid, f[i] - change[i], f[OPP[i]]) for i in range(Q)]


def turned(v, by):
    return pltpu.roll(v, by % 128, 1) if by % 128 else v


def swapped(v):
    return pltpu.roll(v, 4, 0)


def kernel(
    dims, slots_ref, near_ref, pop_ref, mask_ref, out_ref, found, source_of, found_sem, *rest
):
    field, ext, side, stage_e, stage_l, back_e, back_l = rest[:7]
    rest = rest[7:]
    nx, nz, nc = dims
    nd = lax.axis_size("depth")
    per_x = nz * nc * CAP
    layer = lax.axis_index("depth")
    me = lax.axis_index("plane")
    core = me % nc
    z = (me // nc) % nz
    x = me // (nc * nz)
    mine = (z * nc + core) * CAP
    first_slot = me * CAP

    def plane(xx, zz, cc):
        return {"plane": (xx * nz + zz) * nc + cc}

    above = {"depth": (layer + 1) % nd}
    below = {"depth": (layer + nd - 1) % nd}
    ring = [plane(x, (z + far + nz) % nz, core) for far in (-1, 1, -2, 2)]
    twin = plane(x, z, 1 - core)
    across = [plane((x + k) % nx, z, core) for k in range(1, nx)]

    barrier = pltpu.get_barrier_semaphore()
    partners = [above, below, twin] + ring + across
    for other in partners:
        pl.semaphore_signal(barrier, inc=1, device_id=other, device_id_type=MESH)

    send_sems, recv_sems = rest[-2:]
    per_step = rest[:-2]
    used = [0]

    def copy(src, dst, device):
        n = used[0]
        used[0] += 1
        return pltpu.make_async_remote_copy(
            src_ref=src,
            dst_ref=dst,
            send_sem=send_sems.at[n],
            recv_sem=recv_sems.at[n],
            device_id=device,
            device_id_type=MESH,
        )

    lane = lax.broadcasted_iota(jnp.int32, (8, 128), 1)
    tile_row = lax.broadcasted_iota(jnp.int32, (8, 128), 0)
    zin, group = lane % BE, lane // BE
    low_half = tile_row < CAP

    def collide_all(step, up, down):
        for k in range(5):
            up[k] = jnp.zeros((8, 128), F32)
            down[k] = jnp.zeros((8, 128), F32)

        def body(n, carry):
            pair = pl.ds(2 * n, 2)
            if step == 0:
                f = [pop_ref[i, pair] * WEIGHTS[i] for i in range(Q)]
            else:
                f = [field[i, pair] for i in range(Q)]
            post = collided(f, mask_ref[pair] == 1)
            for i in range(Q):
                ext[i, pl.ds(2 * n + 1, 2)] = post[i]
            for j in range(2):
                at = 2 * n + j
                mine = zin == at
                for k, i in enumerate(ZPLUS):
                    moved = pltpu.roll(post[i][j], (at + 113) % 128, 1)
                    up[k] = jnp.where(mine, moved, up[k])
                for k, i in enumerate(ZMINUS):
                    down[k] = jnp.where(mine, pltpu.roll(post[i][j], at, 1), down[k])
            return carry

        lax.fori_loop(0, BE // 2, body, 0)

    def face_x(i):
        return ext[i, BE] if DIRS[i][0] > 0 else ext[i, 1]

    def face_y(i):
        upper = DIRS[i][1] > 0
        halves = []
        for q in range(2):
            part = None
            for k in range(8):
                moved = turned(ext[i, 1 + 8 * q + k], 16 * k + 16 * upper)
                part = moved if part is None else jnp.where(group == k, moved, part)
            halves.append(part)
        if upper:
            return jnp.where(low_half, swapped(halves[0]), halves[1])
        return jnp.where(low_half, halves[0], swapped(halves[1]))

    def by_slot(stage, faces, table):
        for s in range(CAP):
            for f in range(faces):
                table[mine + s, f] = stage[f, pl.ds(s, 8, stride=CAP), :]

    def pack_early(table):
        for f, dirs in enumerate(EARLY):
            for k, i in enumerate(dirs):
                stage_e[f, 8 * k : 8 * k + 8, :] = face_x(i) if f < 2 else face_y(i)
        stage_e[0, 24:32, :] = jnp.where(low_half, swapped(face_x(7)), swapped(face_x(9)))
        stage_e[1, 24:32, :] = jnp.where(low_half, swapped(face_x(10)), swapped(face_x(8)))
        for f in (2, 3):
            stage_e[f, 24:32, :] = jnp.zeros((8, 128), F32)
        by_slot(stage_e, 4, table)

    def shift_z(from_below, from_above, table):
        def body(at, carry):
            for k, i in enumerate(ZPLUS):
                rim = pltpu.roll(from_below[k], (128 - at) % 128, 1)
                ext[i, at + 1] = jnp.where(zin == 0, rim, pltpu.roll(ext[i, at + 1], 1, 1))
            for k, i in enumerate(ZMINUS):
                rim = pltpu.roll(from_above[k], 15 - at, 1)
                ext[i, at + 1] = jnp.where(
                    zin == BE - 1, rim, pltpu.roll(ext[i, at + 1], 127, 1)
                )
            return carry

        lax.fori_loop(0, BE, body, 0)
        for f, dirs in enumerate(LATE):
            for k, i in enumerate(dirs):
                stage_l[f, 8 * k : 8 * k + 8, :] = face_x(i) if f == 0 else face_y(i)
        by_slot(stage_l, 2, table)

    class Gather:
        def __init__(self, table):
            def block(far, first=0, count=CAP):
                start = (((z + far + 2 * nz) % nz) * nc + core) * CAP + first
                return table.at[pl.ds(start, count)]

            def send(far, to, first=0, count=CAP):
                part = block(far, first, count)
                return copy(part, part, plane(x, (z + to + nz) % nz, core))

            def to_twin(far):
                return copy(block(far), block(far), twin)

            self.two = [send(0, -2), send(0, 2)]
            self.one = [send(0, -1), send(0, 1)]
            self.own = to_twin(0)
            self.three = [send(2, -1), send(-2, 1)]
            self.four = [send(2, -2, 0, CAP // 2), send(-2, 2, CAP // 2, CAP // 2)]
            self.twin_one = [to_twin(1), to_twin(-1)]
            self.twin_two = [to_twin(2), to_twin(-2)]
            self.twin_three = [to_twin(3), to_twin(-3)]
            self.twin_four = to_twin(4)

        def begin(self):
            for c in self.two + self.one + [self.own]:
                c.start()

        def forward(self):
            for side in range(2):
                self.two[side].wait_recv()
                self.three[side].start()
                self.four[side].start()
                self.twin_two[side].start()
            for side in range(2):
                self.one[side].wait_recv()
                self.twin_one[side].start()

        def finish(self):
            for side in range(2):
                self.three[side].wait_recv()
                self.twin_three[side].start()
            for side in range(2):
                self.four[side].wait_recv()
            self.twin_four.start()
            for c in self.twin_all():
                c.wait_recv()

        def twin_all(self):
            return [self.own, *self.twin_one, *self.twin_two, *self.twin_three, self.twin_four]

        def sent(self):
            for c in self.two + self.one + self.three + self.four + self.twin_all():
                c.wait_send()

    def source(k, xx, s):
        return source_of[k, xx * per_x + mine + s]

    def early_row(table, to, base, xx):
        def body(s, carry):
            at = [source(k, xx, s) % per_x for k in range(8)]
            for tile, (main, six, seven) in enumerate(((0, 4, 6), (1, 7, 5))):
                got = jnp.where(tile_row == 6, table[at[six], tile], table[at[main], tile])
                to[base + s, tile] = jnp.where(tile_row == 7, table[at[seven], tile], got)
            to[base + s, 2] = table[at[2], 2]
            to[base + s, 3] = table[at[3], 3]
            return carry

        lax.fori_loop(0, CAP, body, 0)

    def late_row(table, to, base, xx):
        def body(s, carry):
            at = [source(k, xx, s) % per_x for k in range(4)]
            for tile in range(2):
                to[base + s, tile] = jnp.where(
                    tile_row < 4, table[at[2 * tile], tile], table[at[2 * tile + 1], tile]
                )
            return carry

        lax.fori_loop(0, CAP, body, 0)

    def hand_out(fill, table, out, got):
        sends = []
        for k in range(1, nx):
            fill(table, out, (k - 1) * CAP, (x + k) % nx)
            c = copy(
                out.at[pl.ds((k - 1) * CAP, CAP)], got.at[pl.ds(x * CAP, CAP)], across[k - 1]
            )
            c.start()
            sends.append(c)
        fill(table, got, x * CAP, x)
        return sends

    def place_halos(early, late):
        for s in range(CAP):
            of = [(source(k, x, s) // per_x) * CAP + s for k in range(8)]
            spread = pl.ds(s, 8, stride=CAP)
            for f, (main, six, seven) in enumerate(((0, 4, 6), (1, 7, 5))):
                got = jnp.where(tile_row == 6, early[of[six], f], early[of[main], f])
                back_e[f, spread, :] = jnp.where(tile_row == 7, early[of[seven], f], got)
            back_e[2, spread, :] = early[of[2], 2]
            back_e[3, spread, :] = early[of[3], 3]
            for f in range(2):
                back_l[f, spread, :] = jnp.where(
                    tile_row < 4, late[of[2 * f], f], late[of[2 * f + 1], f]
                )

        def put_x(i, tile):
            ext[i, 0 if DIRS[i][0] > 0 else BE + 1] = tile

        y_tiles = {}
        for f, dirs in enumerate(EARLY):
            for k, i in enumerate(dirs):
                tile = back_e[f, 8 * k : 8 * k + 8, :]
                if f < 2:
                    put_x(i, tile)
                else:
                    y_tiles[i] = tile
        for k, i in enumerate(LATE[0]):
            put_x(i, back_l[0, 8 * k : 8 * k + 8, :])
        for k, i in enumerate(LATE[1]):
            y_tiles[i] = back_l[1, 8 * k : 8 * k + 8, :]
        for f, ends in enumerate(((7, 9), (10, 8))):
            for i in ends:
                side[YDIRS.index(i), 0 if f == 0 else BE + 1] = back_e[f, 24:32, :]
        for j, i in enumerate(YDIRS):
            upper = DIRS[i][1] > 0
            tile = y_tiles[i]
            other = swapped(tile)
            for at in range(BE):
                part = tile if (at < 8) == upper else other
                side[j, at + 1] = turned(part, (112 if upper else 0) - 16 * (at % 8))

    def shift_xy(last):
        if last:
            held = jnp.zeros((8, 128), jnp.int32)
            for s in range(CAP):
                held = jnp.where(tile_row % CAP == s, source_of[8, first_slot + s], held)

        def body(at, carry):
            for i in range(Q):
                cx, cy, _ = DIRS[i]
                part = ext[i, at + 1 - cx]
                if cy:
                    beside = side[YDIRS.index(i), at + 1 - cx]
                    if cy > 0:
                        beside = jnp.where(low_half, beside, swapped(part))
                        part = pltpu.roll(jnp.where(group == 7, beside, part), BE, 1)
                    else:
                        beside = jnp.where(low_half, swapped(part), beside)
                        part = pltpu.roll(jnp.where(group == 0, beside, part), 128 - BE, 1)
                if last:
                    out_ref[i, at] = jnp.where(held == 1, part * (1.0 / WEIGHTS[i]), 0.0)
                else:
                    field[i, at] = part
            return carry

        lax.fori_loop(0, BE, body, 0)

    for step in range(STEPS):
        up, down, low, high, table_e, table_l, out_e, out_l, got_e, got_l = per_step[
            10 * step : 10 * step + 10
        ]
        collide_all(step, up, down)
        if step == 0:
            pl.semaphore_wait(barrier, len(partners))
        rims = [copy(up, low, above), copy(down, high, below)]
        for c in rims:
            c.start()
        pack_early(table_e)
        early = Gather(table_e)
        early.begin()
        if step == 0:
            find_sources(slots_ref, near_ref, found)
            to_scalars = pltpu.make_async_copy(found, source_of, found_sem)
            to_scalars.start()
            to_scalars.wait()
        for c in rims:
            c.wait_recv()
        shift_z(low, high, table_l)
        late = Gather(table_l)
        late.begin()
        early.forward()
        late.forward()
        early.finish()
        sends = hand_out(early_row, table_e, out_e, got_e)
        late.finish()
        sends += hand_out(late_row, table_l, out_l, got_l)
        for c in sends:
            c.wait_recv()
        place_halos(got_e, got_l)
        shift_xy(step == STEPS - 1)
        early.sent()
        late.sent()
        for c in rims + sends:
            c.wait_send()


def solution(mesh):
    planes = mesh.shape["plane"]
    dims = PLANE_DIMS[planes]
    nx, nz, nc = dims
    group = nz * nc * CAP

    def shards(populations, fluid_mask, block_per_slot, neighbours):
        slots = block_per_slot.shape[0]
        pops = populations[0].reshape(CAP, Q, BE, 2, 128).transpose(1, 2, 3, 0, 4)
        mask = fluid_mask[0].reshape(CAP, BE, 2, 128).transpose(1, 2, 0, 3)
        scratch = [
            pltpu.VMEM((16, slots), jnp.int32),
            pltpu.SMEM((16, slots), jnp.int32),
            pltpu.SemaphoreType.DMA,
            pltpu.VMEM((Q, BE, 8, 128), F32),
            pltpu.VMEM((Q, BE + 2, 8, 128), F32),
            pltpu.VMEM((len(YDIRS), BE + 2, 8, 128), F32),
            pltpu.VMEM((4, 32, 128), F32),
            pltpu.VMEM((2, 32, 128), F32),
            pltpu.VMEM((4, 32, 128), F32),
            pltpu.VMEM((2, 32, 128), F32),
        ]
        for _ in range(STEPS):
            scratch += [pltpu.VMEM((5, 8, 128), F32)] * 4
            for count, tiles in ((group, 4), (group, 2)):
                scratch.append(pltpu.VMEM((count, tiles, 8, 128), F32))
            for tiles in (4, 2):
                scratch.append(pltpu.VMEM(((nx - 1) * CAP, tiles, 8, 128), F32))
            for tiles in (4, 2):
                scratch.append(pltpu.VMEM((nx * CAP, tiles, 8, 128), F32))
        copies = STEPS * (2 + 2 * 16 + 2 * (nx - 1))
        scratch += [pltpu.SemaphoreType.DMA((copies,)), pltpu.SemaphoreType.DMA((copies,))]
        vmem = pl.BlockSpec(memory_space=pltpu.VMEM)
        out = pl.pallas_call(
            functools.partial(kernel, dims),
            out_shape=jax.ShapeDtypeStruct((Q, BE, 8, 128), F32),
            in_specs=[vmem] * 4,
            out_specs=vmem,
            scratch_shapes=scratch,
            compiler_params=pltpu.CompilerParams(
                collective_id=0, has_side_effects=True, vmem_limit_bytes=40 * 1024 * 1024
            ),
        )(
            block_per_slot.reshape(1, slots),
            neighbours.T,
            pops.reshape(Q, BE, 8, 128),
            mask.reshape(BE, 8, 128),
        )
        out = out.reshape(Q, BE, 2, CAP, 128).transpose(3, 0, 1, 2, 4)
        return out.reshape(populations.shape)

    return jax.shard_map(
        shards,
        mesh=mesh,
        in_specs=(P("depth", "plane", None, None), P("depth", "plane", None), P(), P()),
        out_specs=P("depth", "plane", None, None),
        check_vma=False,
    )
```

time: 76.6 us -> 64.3 us (0.84)
  Pallas kernels: 71 us -> 59.5 us
  local copies, waits for them, and re-layouts: 5.32 us -> 4.53 us
    pallas_call x1, Pallas kernels: 68.4 us -> 59.5 us  [shards(): pl.pallas_call(functools.partial(kernel, dims), out_shape=jax.ShapeDtypeS...]
    pallas_call x1 -> x0, Pallas kernels: 2.63 us -> none  [shards(): pl.pallas_call(sources_kernel, out_shape=jax.ShapeDtypeStruct((16, slots)...]
    pallas_call x1 -> x0, local copies, waits for them, and re-layouts: 1.84 us -> none  [shards(): pl.pallas_call(functools.partial(kernel, dims), out_shape=jax.ShapeDtypeS...]
    unnamed x6 -> x9, local copies, waits for them, and re-layouts: 3.49 us -> 4.53 us
where the time goes in v2:
time: 64.3 us; the launch traced here: 64.1 us
  Pallas kernels  59.5 us (93%)
  local copies, waits for them, and re-layouts  4.53 us (7%)
    pallas_call x1, Pallas kernels, shards(): pl.pallas_call(functools.partial(kernel, dims), out_shape=jax.ShapeDtypeS...  59.5 us
    unnamed x9, local copies, waits for them, and re-layouts  4.53 us

profile of v2, /device:TPU:1, one launch (start us, length us, event | category | flops | bytes accessed | tf_op | source)
XLA Modules:
  0.0 64.1 jit_solution(15097976031339846944)
XLA Ops:
  0.0 0.0 copy-start
  0.0 1.3 %copy-done = f32[1,4,19,4096]{3,1,2,0:T(4,128)S(1)} copy-done((f32[1,4,19,4096]{3,1,2,0:T(4,128)S(1)}, f32[1,4,19,4096]{3,1,2,0:T(4,128)}, u32[]{:S(2)}) %copy-start) | copy-done | bytes 1245208
  1.3 0.0 copy-start.1
  1.3 0.8 %copy-done.1 = s32[1,4,4096]{2,1,0:T(4,128)S(1)} copy-done((s32[1,4,4096]{2,1,0:T(4,128)S(1)}, s32[1,4,4096]{2,1,0:T(4,128)}, u32[]{:S(2)}) %copy-start.1) | copy-done | bytes 65560
  2.1 0.0 copy-start.2
  2.1 0.7 %copy-done.2 = s32[128,4]{0,1:T(4,128)S(1)} copy-done((s32[128,4]{0,1:T(4,128)S(1)}, s32[128,4]{0,1:T(4,128)}, u32[]{:S(2)}) %copy-start.2) | copy-done | bytes 2072
  2.8 0.0 copy-start.3
  2.8 0.7 %copy-done.3 = s32[256]{0:T(256)S(1)} copy-done((s32[256]{0:T(256)S(1)}, s32[256]{0:T(256)}, u32[]{:S(2)}) %copy-start.3) | copy-done | bytes 1048
  3.5 59.5 %shard_map.46 = f32[19,16,8,128]{3,2,1,0:T(8,128)S(1)} custom-call(s32[1,256]{1,0:T(1,128)S(1)} %bitcast.21, s32[4,128]{1,0:T(4,128)S(1)} %bitcast.20, f32[19,16,8,128]{3,2,1,0:T(8,128)S(1)} %bitcast.18, s32[16,8,128]{2,1,0:T(8,128)S(1)} %bitcast.19), custom_call_target="tpu_custom_call" | custom-call | tf_op jit(solution)/shard_map/pallas_call | solution.py:525
  63.0 1.0 %copy.9 = f32[1,4,19,4096]{3,1,2,0:T(4,128)} copy(f32[1,4,19,4096]{3,1,2,0:T(4,128)S(1)} %bitcast.17) | data formatting | bytes 2490368
Async XLA Ops:
  0.0 1.3 %copy-start = (f32[1,4,19,4096]{3,1,2,0:T(4,128)S(1)}, f32[1,4,19,4096]{3,1,2,0:T(4,128)}, u32[]{:S(2)}) copy-start(f32[1,4,19,4096]{3,1,2,0:T(4,128)} %param.4) | copy-start | bytes 3735556
  1.3 0.8 %copy-start.1 = (s32[1,4,4096]{2,1,0:T(4,128)S(1)}, s32[1,4,4096]{2,1,0:T(4,128)}, u32[]{:S(2)}) copy-start(s32[1,4,4096]{2,1,0:T(4,128)} %param.5) | copy-start | bytes 196612
  2.1 0.7 %copy-start.2 = (s32[128,4]{0,1:T(4,128)S(1)}, s32[128,4]{0,1:T(4,128)}, u32[]{:S(2)}) copy-start(s32[128,4]{0,1:T(4,128)} %param.7) | copy-start | bytes 6148
  2.8 0.7 %copy-start.3 = (s32[256]{0:T(256)S(1)}, s32[256]{0:T(256)}, u32[]{:S(2)}) copy-start(s32[256]{0:T(256)} %param.6) | copy-start | bytes 3076

commit v3 on v2

--- a/solution.py
+++ b/solution.py
@@ -40,8 +40,7 @@
 WEIGHTS = [1.0 / 3.0] + [1.0 / 18.0] * 6 + [1.0 / 36.0] * 12
 ZPLUS = [5, 11, 14, 15, 18]
 ZMINUS = [6, 12, 13, 16, 17]
-EARLY = ((1, 7, 9), (2, 8, 10), (3, 7, 10), (4, 8, 9))
-LATE = ((11, 13, 12, 14), (15, 17, 16, 18))
+CHUNKS = (((1, 7, 9), (2, 8, 10)), ((3, 7, 10), (4, 8, 9)), ((11, 13, 12, 14), (15, 17, 16, 18)))
 YDIRS = [i for i in range(Q) if DIRS[i][1] != 0]
 
 
@@ -167,10 +166,10 @@
 
 
 def kernel(
-    dims, slots_ref, near_ref, pop_ref, mask_ref, out_ref, found, source_of, found_sem, *rest
+    dims, slots_in, near_in, pop_in, mask_in, out_ref, found, source_of, found_sem, *rest
 ):
-    field, ext, side, stage_e, stage_l, back_e, back_l = rest[:7]
-    rest = rest[7:]
+    slots_ref, near_ref, pop_ref, mask_ref, in_sems, ext_a, ext_b, side, stage, back = rest[:10]
+    rest = rest[10:]
     nx, nz, nc = dims
     nd = lax.axis_size("depth")
     per_x = nz * nc * CAP
@@ -195,6 +194,20 @@
     partners = [above, below, twin] + ring + across
     for other in partners:
         pl.semaphore_signal(barrier, inc=1, device_id=other, device_id_type=MESH)
+
+    arguments = [
+        pltpu.make_async_copy(src, dst, in_sems.at[n])
+        for n, (src, dst) in enumerate(
+            (
+                (slots_in, slots_ref),
+                (near_in, near_ref),
+                (mask_in, mask_ref),
+                (pop_in, pop_ref),
+            )
+        )
+    ]
+    for c in arguments:
+        c.start()
 
     send_sems, recv_sems = rest[-2:]
     per_step = rest[:-2]
@@ -217,36 +230,56 @@
     zin, group = lane % BE, lane // BE
     low_half = tile_row < CAP
 
-    def collide_all(step, up, down):
+    def streamed(ext, at):
+        parts = []
+        for i in range(Q):
+            cx, cy, _ = DIRS[i]
+            part = ext[i, at + 1 - cx]
+            if cy:
+                beside = side[YDIRS.index(i), at + 1 - cx]
+                if cy > 0:
+                    beside = jnp.where(low_half, beside, swapped(part))
+                    part = pltpu.roll(jnp.where(group == 7, beside, part), BE, 1)
+                else:
+                    beside = jnp.where(low_half, swapped(part), beside)
+                    part = pltpu.roll(jnp.where(group == 0, beside, part), 128 - BE, 1)
+            parts.append(part)
+        return parts
+
+    def collide(at, old, into, up, down):
+        if old is None:
+            f = [pop_ref[i, at] * WEIGHTS[i] for i in range(Q)]
+        else:
+            f = streamed(old, at)
+        post = collided(f, mask_ref[at] == 1)
+        for i in range(Q):
+            into[i, at + 1] = post[i]
+        mine = zin == at
+        for k, i in enumerate(ZPLUS):
+            up[k] = jnp.where(mine, pltpu.roll(post[i], (at + 113) % 128, 1), up[k])
+        for k, i in enumerate(ZMINUS):
+            down[k] = jnp.where(mine, pltpu.roll(post[i], at, 1), down[k])
+
+    def collide_ends(*to):
+        up, down = to[-2:]
         for k in range(5):
             up[k] = jnp.zeros((8, 128), F32)
             down[k] = jnp.zeros((8, 128), F32)
-
+        for at in (0, BE - 1):
+            collide(at, *to)
+
+    def collide_rest(*to):
         def body(n, carry):
-            pair = pl.ds(2 * n, 2)
-            if step == 0:
-                f = [pop_ref[i, pair] * WEIGHTS[i] for i in range(Q)]
-            else:
-                f = [field[i, pair] for i in range(Q)]
-            post = collided(f, mask_ref[pair] == 1)
-            for i in range(Q):
-                ext[i, pl.ds(2 * n + 1, 2)] = post[i]
-            for j in range(2):
-                at = 2 * n + j
-                mine = zin == at
-                for k, i in enumerate(ZPLUS):
-                    moved = pltpu.roll(post[i][j], (at + 113) % 128, 1)
-                    up[k] = jnp.where(mine, moved, up[k])
-                for k, i in enumerate(ZMINUS):
-                    down[k] = jnp.where(mine, pltpu.roll(post[i][j], at, 1), down[k])
+            collide(n, *to)
+            collide(BE - 1 - n, *to)
             return carry
 
-        lax.fori_loop(0, BE // 2, body, 0)
-
-    def face_x(i):
+        lax.fori_loop(1, BE // 2, body, 0)
+
+    def face_x(ext, i):
         return ext[i, BE] if DIRS[i][0] > 0 else ext[i, 1]
 
-    def face_y(i):
+    def face_y(ext, i):
         upper = DIRS[i][1] > 0
         halves = []
         for q in range(2):
@@ -259,22 +292,25 @@
             return jnp.where(low_half, swapped(halves[0]), halves[1])
         return jnp.where(low_half, halves[0], swapped(halves[1]))
 
-    def by_slot(stage, faces, table):
+    def pack(chunk, ext, table):
+        for f, dirs in enumerate(CHUNKS[chunk]):
+            for k, i in enumerate(dirs):
+                along_x = chunk == 0 or (chunk == 2 and f == 0)
+                stage[chunk, f, 8 * k : 8 * k + 8, :] = (
+                    face_x(ext, i) if along_x else face_y(ext, i)
+                )
+        if chunk == 0:
+            for f, (i, j) in enumerate(((7, 9), (10, 8))):
+                ends = jnp.where(low_half, swapped(face_x(ext, i)), swapped(face_x(ext, j)))
+                stage[chunk, f, 24:32, :] = ends
+        if chunk == 1:
+            for f in range(2):
+                stage[chunk, f, 24:32, :] = jnp.zeros((8, 128), F32)
         for s in range(CAP):
-            for f in range(faces):
-                table[mine + s, f] = stage[f, pl.ds(s, 8, stride=CAP), :]
-
-    def pack_early(table):
-        for f, dirs in enumerate(EARLY):
-            for k, i in enumerate(dirs):
-                stage_e[f, 8 * k : 8 * k + 8, :] = face_x(i) if f < 2 else face_y(i)
-        stage_e[0, 24:32, :] = jnp.where(low_half, swapped(face_x(7)), swapped(face_x(9)))
-        stage_e[1, 24:32, :] = jnp.where(low_half, swapped(face_x(10)), swapped(face_x(8)))
-        for f in (2, 3):
-            stage_e[f, 24:32, :] = jnp.zeros((8, 128), F32)
-        by_slot(stage_e, 4, table)
-
-    def shift_z(from_below, from_above, table):
+            for f in range(2):
+                table[mine + s, f] = stage[chunk, f, pl.ds(s, 8, stride=CAP), :]
+
+    def shift_z(ext, from_below, from_above):
         def body(at, carry):
             for k, i in enumerate(ZPLUS):
                 rim = pltpu.roll(from_below[k], (128 - at) % 128, 1)
@@ -287,10 +323,6 @@
             return carry
 
         lax.fori_loop(0, BE, body, 0)
-        for f, dirs in enumerate(LATE):
-            for k, i in enumerate(dirs):
-                stage_l[f, 8 * k : 8 * k + 8, :] = face_x(i) if f == 0 else face_y(i)
-        by_slot(stage_l, 2, table)
 
     class Gather:
         def __init__(self, table):
@@ -329,13 +361,15 @@
                 self.one[side].wait_recv()
                 self.twin_one[side].start()
 
-        def finish(self):
+        def pass_on(self):
             for side in range(2):
                 self.three[side].wait_recv()
                 self.twin_three[side].start()
             for side in range(2):
                 self.four[side].wait_recv()
             self.twin_four.start()
+
+        def finish(self):
             for c in self.twin_all():
                 c.wait_recv()
 
@@ -349,143 +383,128 @@
     def source(k, xx, s):
         return source_of[k, xx * per_x + mine + s]
 
-    def early_row(table, to, base, xx):
+    def merged(chunk, f, read):
+        if chunk == 0:
+            main, six, seven = ((0, 4, 6), (1, 7, 5))[f]
+            got = jnp.where(tile_row == 6, read(six, f), read(main, f))
+            return jnp.where(tile_row == 7, read(seven, f), got)
+        if chunk == 1:
+            return read(2 + f, f)
+        return jnp.where(tile_row < 4, read(2 * f, f), read(2 * f + 1, f))
+
+    def choose(chunk, table, to, base, xx):
         def body(s, carry):
-            at = [source(k, xx, s) % per_x for k in range(8)]
-            for tile, (main, six, seven) in enumerate(((0, 4, 6), (1, 7, 5))):
-                got = jnp.where(tile_row == 6, table[at[six], tile], table[at[main], tile])
-                to[base + s, tile] = jnp.where(tile_row == 7, table[at[seven], tile], got)
-            to[base + s, 2] = table[at[2], 2]
-            to[base + s, 3] = table[at[3], 3]
-            return carry
-
-        lax.fori_loop(0, CAP, body, 0)
-
-    def late_row(table, to, base, xx):
-        def body(s, carry):
-            at = [source(k, xx, s) % per_x for k in range(4)]
-            for tile in range(2):
-                to[base + s, tile] = jnp.where(
-                    tile_row < 4, table[at[2 * tile], tile], table[at[2 * tile + 1], tile]
+            for f in range(2):
+                to[base + s, f] = merged(
+                    chunk, f, lambda k, f: table[source(k, xx, s) % per_x, f]
                 )
             return carry
 
         lax.fori_loop(0, CAP, body, 0)
 
-    def hand_out(fill, table, out, got):
+    def hand_out(chunk, table, out, got):
         sends = []
         for k in range(1, nx):
-            fill(table, out, (k - 1) * CAP, (x + k) % nx)
+            choose(chunk, table, out, (k - 1) * CAP, (x + k) % nx)
             c = copy(
                 out.at[pl.ds((k - 1) * CAP, CAP)], got.at[pl.ds(x * CAP, CAP)], across[k - 1]
             )
             c.start()
             sends.append(c)
-        fill(table, got, x * CAP, x)
+        choose(chunk, table, got, x * CAP, x)
         return sends
 
-    def place_halos(early, late):
+    def place_halos(chunk, ext, got):
         for s in range(CAP):
-            of = [(source(k, x, s) // per_x) * CAP + s for k in range(8)]
-            spread = pl.ds(s, 8, stride=CAP)
-            for f, (main, six, seven) in enumerate(((0, 4, 6), (1, 7, 5))):
-                got = jnp.where(tile_row == 6, early[of[six], f], early[of[main], f])
-                back_e[f, spread, :] = jnp.where(tile_row == 7, early[of[seven], f], got)
-            back_e[2, spread, :] = early[of[2], 2]
-            back_e[3, spread, :] = early[of[3], 3]
             for f in range(2):
-                back_l[f, spread, :] = jnp.where(
-                    tile_row < 4, late[of[2 * f], f], late[of[2 * f + 1], f]
+                back[chunk, f, pl.ds(s, 8, stride=CAP), :] = merged(
+                    chunk, f, lambda k, f: got[(source(k, x, s) // per_x) * CAP + s, f]
                 )
-
-        def put_x(i, tile):
-            ext[i, 0 if DIRS[i][0] > 0 else BE + 1] = tile
-
-        y_tiles = {}
-        for f, dirs in enumerate(EARLY):
+        for f, dirs in enumerate(CHUNKS[chunk]):
             for k, i in enumerate(dirs):
-                tile = back_e[f, 8 * k : 8 * k + 8, :]
-                if f < 2:
-                    put_x(i, tile)
-                else:
-                    y_tiles[i] = tile
-        for k, i in enumerate(LATE[0]):
-            put_x(i, back_l[0, 8 * k : 8 * k + 8, :])
-        for k, i in enumerate(LATE[1]):
-            y_tiles[i] = back_l[1, 8 * k : 8 * k + 8, :]
-        for f, ends in enumerate(((7, 9), (10, 8))):
-            for i in ends:
-                side[YDIRS.index(i), 0 if f == 0 else BE + 1] = back_e[f, 24:32, :]
-        for j, i in enumerate(YDIRS):
-            upper = DIRS[i][1] > 0
-            tile = y_tiles[i]
-            other = swapped(tile)
-            for at in range(BE):
-                part = tile if (at < 8) == upper else other
-                side[j, at + 1] = turned(part, (112 if upper else 0) - 16 * (at % 8))
-
-    def shift_xy(last):
-        if last:
-            held = jnp.zeros((8, 128), jnp.int32)
-            for s in range(CAP):
-                held = jnp.where(tile_row % CAP == s, source_of[8, first_slot + s], held)
+                tile = back[chunk, f, 8 * k : 8 * k + 8, :]
+                if chunk == 0 or (chunk == 2 and f == 0):
+                    ext[i, 0 if DIRS[i][0] > 0 else BE + 1] = tile
+                    continue
+                upper = DIRS[i][1] > 0
+                other = swapped(tile)
+                for at in range(BE):
+                    part = tile if (at < 8) == upper else other
+                    side[YDIRS.index(i), at + 1] = turned(
+                        part, (112 if upper else 0) - 16 * (at % 8)
+                    )
+        if chunk == 0:
+            for f, ends in enumerate(((7, 9), (10, 8))):
+                for i in ends:
+                    side[YDIRS.index(i), 0 if f == 0 else BE + 1] = back[0, f, 24:32, :]
+
+    def give_out(ext):
+        held = jnp.zeros((8, 128), jnp.int32)
+        for s in range(CAP):
+            held = jnp.where(tile_row % CAP == s, source_of[8, first_slot + s], held)
 
         def body(at, carry):
-            for i in range(Q):
-                cx, cy, _ = DIRS[i]
-                part = ext[i, at + 1 - cx]
-                if cy:
-                    beside = side[YDIRS.index(i), at + 1 - cx]
-                    if cy > 0:
-                        beside = jnp.where(low_half, beside, swapped(part))
-                        part = pltpu.roll(jnp.where(group == 7, beside, part), BE, 1)
-                    else:
-                        beside = jnp.where(low_half, swapped(part), beside)
-                        part = pltpu.roll(jnp.where(group == 0, beside, part), 128 - BE, 1)
-                if last:
-                    out_ref[i, at] = jnp.where(held == 1, part * (1.0 / WEIGHTS[i]), 0.0)
-                else:
-                    field[i, at] = part
+            for i, part in enumerate(streamed(ext, at)):
+                out_ref[i, at] = jnp.where(held == 1, part * (1.0 / WEIGHTS[i]), 0.0)
             return carry
 
         lax.fori_loop(0, BE, body, 0)
 
     for step in range(STEPS):
-        up, down, low, high, table_e, table_l, out_e, out_l, got_e, got_l = per_step[
-            10 * step : 10 * step + 10
-        ]
-        collide_all(step, up, down)
+        up, down, low, high, *buffers = per_step[13 * step : 13 * step + 13]
+        tables, outs, gots = buffers[0:3], buffers[3:6], buffers[6:9]
+        old, ext = (ext_b, ext_a) if step % 2 == 0 else (ext_a, ext_b)
+        first, second, third = [Gather(table) for table in tables]
+        to = (None if step == 0 else old, ext, up, down)
         if step == 0:
-            pl.semaphore_wait(barrier, len(partners))
-        rims = [copy(up, low, above), copy(down, high, below)]
-        for c in rims:
-            c.start()
-        pack_early(table_e)
-        early = Gather(table_e)
-        early.begin()
+            for c in arguments:
+                c.wait()
+        collide_ends(*to)
         if step == 0:
+            collide_rest(*to)
             find_sources(slots_ref, near_ref, found)
             to_scalars = pltpu.make_async_copy(found, source_of, found_sem)
             to_scalars.start()
             to_scalars.wait()
+            pl.semaphore_wait(barrier, len(partners))
+        rims = [copy(up, low, above), copy(down, high, below)]
+        if step == 0:
+            for c in rims:
+                c.start()
+        pack(0, ext, tables[0])
+        first.begin()
+        if step > 0:
+            collide_rest(*to)
+            for c in rims:
+                c.start()
+        pack(1, ext, tables[1])
+        second.begin()
         for c in rims:
             c.wait_recv()
-        shift_z(low, high, table_l)
-        late = Gather(table_l)
-        late.begin()
-        early.forward()
-        late.forward()
-        early.finish()
-        sends = hand_out(early_row, table_e, out_e, got_e)
-        late.finish()
-        sends += hand_out(late_row, table_l, out_l, got_l)
-        for c in sends:
-            c.wait_recv()
-        place_halos(got_e, got_l)
-        shift_xy(step == STEPS - 1)
-        early.sent()
-        late.sent()
-        for c in rims + sends:
+        shift_z(ext, low, high)
+        pack(2, ext, tables[2])
+        third.begin()
+        first.forward()
+        second.forward()
+        third.forward()
+        first.pass_on()
+        first.finish()
+        sends = [hand_out(0, tables[0], outs[0], gots[0])]
+        second.pass_on()
+        second.finish()
+        sends.append(hand_out(1, tables[1], outs[1], gots[1]))
+        third.pass_on()
+        third.finish()
+        sends.append(hand_out(2, tables[2], outs[2], gots[2]))
+        for chunk in range(3):
+            for c in sends[chunk]:
+                c.wait_recv()
+            place_halos(chunk, ext, gots[chunk])
+        if step == STEPS - 1:
+            give_out(ext)
+        for gather in (first, second, third):
+            gather.sent()
+        for c in rims + sum(sends, []):
             c.wait_send()
 
 
@@ -503,39 +522,43 @@
             pltpu.VMEM((16, slots), jnp.int32),
             pltpu.SMEM((16, slots), jnp.int32),
             pltpu.SemaphoreType.DMA,
+            pltpu.VMEM((1, slots), jnp.int32),
+            pltpu.VMEM(neighbours.shape[::-1], jnp.int32),
             pltpu.VMEM((Q, BE, 8, 128), F32),
+            pltpu.VMEM((BE, 8, 128), jnp.int32),
+            pltpu.SemaphoreType.DMA((4,)),
+            pltpu.VMEM((Q, BE + 2, 8, 128), F32),
             pltpu.VMEM((Q, BE + 2, 8, 128), F32),
             pltpu.VMEM((len(YDIRS), BE + 2, 8, 128), F32),
-            pltpu.VMEM((4, 32, 128), F32),
-            pltpu.VMEM((2, 32, 128), F32),
-            pltpu.VMEM((4, 32, 128), F32),
-            pltpu.VMEM((2, 32, 128), F32),
+            pltpu.VMEM((3, 2, 32, 128), F32),
+            pltpu.VMEM((3, 2, 32, 128), F32),
         ]
         for _ in range(STEPS):
             scratch += [pltpu.VMEM((5, 8, 128), F32)] * 4
-            for count, tiles in ((group, 4), (group, 2)):
-                scratch.append(pltpu.VMEM((count, tiles, 8, 128), F32))
-            for tiles in (4, 2):
-                scratch.append(pltpu.VMEM(((nx - 1) * CAP, tiles, 8, 128), F32))
-            for tiles in (4, 2):
-                scratch.append(pltpu.VMEM((nx * CAP, tiles, 8, 128), F32))
-        copies = STEPS * (2 + 2 * 16 + 2 * (nx - 1))
+            for count in (group, (nx - 1) * CAP, nx * CAP):
+                scratch += [pltpu.VMEM((count, 2, 8, 128), F32)] * 3
+        copies = STEPS * (2 + 3 * (16 + nx - 1))
         scratch += [pltpu.SemaphoreType.DMA((copies,)), pltpu.SemaphoreType.DMA((copies,))]
         vmem = pl.BlockSpec(memory_space=pltpu.VMEM)
         out = pl.pallas_call(
             functools.partial(kernel, dims),
             out_shape=jax.ShapeDtypeStruct((Q, BE, 8, 128), F32),
-            in_specs=[vmem] * 4,
+            in_specs=[pl.BlockSpec(memory_space=pltpu.HBM)] * 4,
             out_specs=vmem,
             scratch_shapes=scratch,
             compiler_params=pltpu.CompilerParams(
                 collective_id=0, has_side_effects=True, vmem_limit_bytes=40 * 1024 * 1024
             ),
         )(
-            block_per_slot.reshape(1, slots),
-            neighbours.T,
-            pops.reshape(Q, BE, 8, 128),
-            mask.reshape(BE, 8, 128),
+            *(
+                pltpu.with_memory_space_constraint(a, pltpu.HBM)
+                for a in (
+                    block_per_slot.reshape(1, slots),
+                    neighbours.T,
+                    pops.reshape(Q, BE, 8, 128),
+                    mask.reshape(BE, 8, 128),
+                )
+            )
         )
         out = out.reshape(Q, BE, 2, CAP, 128).transpose(3, 0, 1, 2, 4)
         return out.reshape(populations.shape)

time: 64.3 us -> 60.9 us (0.947)
  local copies, waits for them, and re-layouts: 4.53 us -> 1.04 us
    unnamed x9 -> x1, local copies, waits for them, and re-layouts: 4.53 us -> 1.04 us
where the time goes in v3:
time: 60.9 us; the launch traced here: 60.8 us
  Pallas kernels  59.7 us (98%)
  local copies, waits for them, and re-layouts  1.04 us (2%)
    pallas_call x1, Pallas kernels, shards(): pl.pallas_call(functools.partial(kernel, dims), out_shape=jax.ShapeDtypeS...  59.7 us

profile of v3, /device:TPU:1, one launch (start us, length us, event | category | flops | bytes accessed | tf_op | source)
XLA Modules:
  0.0 60.8 jit_solution(6454829215444433199)
XLA Ops:
  0.0 59.7 %shard_map.46 = f32[19,16,8,128]{3,2,1,0:T(8,128)S(1)} custom-call(s32[1,256]{1,0:T(1,128)} %bitcast.21, s32[4,128]{1,0:T(4,128)} %bitcast.20, f32[19,16,8,128]{3,2,1,0:T(8,128)} %bitcast.18, s32[16,8,128]{2,1,0:T(8,128)} %bitcast.19), custom_call_target="tpu_custom_call" | custom-call | tf_op jit(solution)/shard_map/pallas_call | solution.py:543
  59.7 1.0 %copy.9 = f32[1,4,19,4096]{3,1,2,0:T(4,128)} copy(f32[1,4,19,4096]{3,1,2,0:T(4,128)S(1)} %bitcast.17) | data formatting | bytes 2490368

commit v4 on v3

--- a/solution.py
+++ b/solution.py
@@ -79,7 +79,7 @@
         hit = jnp.broadcast_to(held[:, part], (blocks, 128)) == down
         for k in range(8):
             out_ref[k : k + 1, part] = top_rows(jnp.where(hit, found[k], 0))[0:1]
-        out_ref[8:16, part] = jnp.broadcast_to(
+        out_ref[16:24, part] = jnp.broadcast_to(
             jnp.where(held[:, part] < blocks, 1, 0), (8, 128)
         )
 
@@ -179,6 +179,7 @@
     z = (me // nc) % nz
     x = me // (nc * nz)
     mine = (z * nc + core) * CAP
+    home = (core * nz + 2) * CAP
     first_slot = me * CAP
 
     def plane(xx, zz, cc):
@@ -187,13 +188,13 @@
     above = {"depth": (layer + 1) % nd}
     below = {"depth": (layer + nd - 1) % nd}
     ring = [plane(x, (z + far + nz) % nz, core) for far in (-1, 1, -2, 2)]
-    twin = plane(x, z, 1 - core)
+    other = plane(x, z, 1 - core)
     across = [plane((x + k) % nx, z, core) for k in range(1, nx)]
 
     barrier = pltpu.get_barrier_semaphore()
-    partners = [above, below, twin] + ring + across
-    for other in partners:
-        pl.semaphore_signal(barrier, inc=1, device_id=other, device_id_type=MESH)
+    partners = [above, below, other] + ring + across
+    for partner in partners:
+        pl.semaphore_signal(barrier, inc=1, device_id=partner, device_id_type=MESH)
 
     arguments = [
         pltpu.make_async_copy(src, dst, in_sems.at[n])
@@ -308,7 +309,7 @@
                 stage[chunk, f, 24:32, :] = jnp.zeros((8, 128), F32)
         for s in range(CAP):
             for f in range(2):
-                table[mine + s, f] = stage[chunk, f, pl.ds(s, 8, stride=CAP), :]
+                table[home + s, f] = stage[chunk, f, pl.ds(s, 8, stride=CAP), :]
 
     def shift_z(ext, from_below, from_above):
         def body(at, carry):
@@ -326,62 +327,53 @@
 
     class Gather:
         def __init__(self, table):
-            def block(far, first=0, count=CAP):
-                start = (((z + far + 2 * nz) % nz) * nc + core) * CAP + first
-                return table.at[pl.ds(start, count)]
-
-            def send(far, to, first=0, count=CAP):
-                part = block(far, first, count)
-                return copy(part, part, plane(x, (z + to + nz) % nz, core))
-
-            def to_twin(far):
-                return copy(block(far), block(far), twin)
+            def block(place, count=1):
+                return table.at[pl.ds((core * nz + place) * CAP, count * CAP)]
+
+            def send(far, to):
+                there = plane(x, (z + to + nz) % nz, core)
+                return copy(block((far + 2) % nz), block((far - to + 2) % nz), there)
 
             self.two = [send(0, -2), send(0, 2)]
             self.one = [send(0, -1), send(0, 1)]
-            self.own = to_twin(0)
             self.three = [send(2, -1), send(-2, 1)]
-            self.four = [send(2, -2, 0, CAP // 2), send(-2, 2, CAP // 2, CAP // 2)]
-            self.twin_one = [to_twin(1), to_twin(-1)]
-            self.twin_two = [to_twin(2), to_twin(-2)]
-            self.twin_three = [to_twin(3), to_twin(-3)]
-            self.twin_four = to_twin(4)
+            way = 1 - 2 * core
+            there = plane(x, (z - 2 * way + nz) % nz, core)
+            self.four = copy(block(2 * way + 2), block(6), there)
+            self.twin = [copy(block(0, 5), block(0, 5), other), copy(block(5, 3), block(5, 3), other)]
 
         def begin(self):
-            for c in self.two + self.one + [self.own]:
+            for c in self.two + self.one:
                 c.start()
 
         def forward(self):
             for side in range(2):
                 self.two[side].wait_recv()
                 self.three[side].start()
-                self.four[side].start()
-                self.twin_two[side].start()
-            for side in range(2):
-                self.one[side].wait_recv()
-                self.twin_one[side].start()
+            self.four.start()
+            for c in self.one:
+                c.wait_recv()
+            self.twin[0].start()
 
         def pass_on(self):
-            for side in range(2):
-                self.three[side].wait_recv()
-                self.twin_three[side].start()
-            for side in range(2):
-                self.four[side].wait_recv()
-            self.twin_four.start()
+            for c in self.three:
+                c.wait_recv()
+            self.four.wait_recv()
+            self.twin[1].start()
 
         def finish(self):
-            for c in self.twin_all():
+            for c in self.twin:
                 c.wait_recv()
 
-        def twin_all(self):
-            return [self.own, *self.twin_one, *self.twin_two, *self.twin_three, self.twin_four]
-
         def sent(self):
-            for c in self.two + self.one + self.three + self.four + self.twin_all():
+            for c in self.two + self.one + self.three + [self.four] + self.twin:
                 c.wait_send()
 
+    def x_of(k, s):
+        return source_of[k, x * per_x + mine + s]
+
     def source(k, xx, s):
-        return source_of[k, xx * per_x + mine + s]
+        return source_of[8 + k, xx * per_x + mine + s]
 
     def merged(chunk, f, read):
         if chunk == 0:
@@ -396,7 +388,7 @@
         def body(s, carry):
             for f in range(2):
                 to[base + s, f] = merged(
-                    chunk, f, lambda k, f: table[source(k, xx, s) % per_x, f]
+                    chunk, f, lambda k, f: table[source(k, xx, s), f]
                 )
             return carry
 
@@ -418,7 +410,7 @@
         for s in range(CAP):
             for f in range(2):
                 back[chunk, f, pl.ds(s, 8, stride=CAP), :] = merged(
-                    chunk, f, lambda k, f: got[(source(k, x, s) // per_x) * CAP + s, f]
+                    chunk, f, lambda k, f: got[x_of(k, s) * CAP + s, f]
                 )
         for f, dirs in enumerate(CHUNKS[chunk]):
             for k, i in enumerate(dirs):
@@ -427,9 +419,9 @@
                     ext[i, 0 if DIRS[i][0] > 0 else BE + 1] = tile
                     continue
                 upper = DIRS[i][1] > 0
-                other = swapped(tile)
+                flipped = swapped(tile)
                 for at in range(BE):
-                    part = tile if (at < 8) == upper else other
+                    part = tile if (at < 8) == upper else flipped
                     side[YDIRS.index(i), at + 1] = turned(
                         part, (112 if upper else 0) - 16 * (at % 8)
                     )
@@ -441,7 +433,7 @@
     def give_out(ext):
         held = jnp.zeros((8, 128), jnp.int32)
         for s in range(CAP):
-            held = jnp.where(tile_row % CAP == s, source_of[8, first_slot + s], held)
+            held = jnp.where(tile_row % CAP == s, source_of[16, first_slot + s], held)
 
         def body(at, carry):
             for i, part in enumerate(streamed(ext, at)):
@@ -463,6 +455,11 @@
         if step == 0:
             collide_rest(*to)
             find_sources(slots_ref, near_ref, found)
+            slot = found[0:8, :]
+            ring = slot % per_x // CAP
+            place = ring % nc * nz + (ring // nc + nz + 2 - z) % nz
+            found[0:8, :] = slot // per_x
+            found[8:16, :] = place * CAP + slot % CAP
             to_scalars = pltpu.make_async_copy(found, source_of, found_sem)
             to_scalars.start()
             to_scalars.wait()
@@ -519,8 +516,8 @@
         pops = populations[0].reshape(CAP, Q, BE, 2, 128).transpose(1, 2, 3, 0, 4)
         mask = fluid_mask[0].reshape(CAP, BE, 2, 128).transpose(1, 2, 0, 3)
         scratch = [
-            pltpu.VMEM((16, slots), jnp.int32),
-            pltpu.SMEM((16, slots), jnp.int32),
+            pltpu.VMEM((24, slots), jnp.int32),
+            pltpu.SMEM((24, slots), jnp.int32),
             pltpu.SemaphoreType.DMA,
             pltpu.VMEM((1, slots), jnp.int32),
             pltpu.VMEM(neighbours.shape[::-1], jnp.int32),
@@ -537,7 +534,7 @@
             scratch += [pltpu.VMEM((5, 8, 128), F32)] * 4
             for count in (group, (nx - 1) * CAP, nx * CAP):
                 scratch += [pltpu.VMEM((count, 2, 8, 128), F32)] * 3
-        copies = STEPS * (2 + 3 * (16 + nx - 1))
+        copies = STEPS * (2 + 3 * (9 + nx - 1))
         scratch += [pltpu.SemaphoreType.DMA((copies,)), pltpu.SemaphoreType.DMA((copies,))]
         vmem = pl.BlockSpec(memory_space=pltpu.VMEM)
         out = pl.pallas_call(

time: 60.9 us -> 58.7 us (0.964)
  Pallas kernels: 59.7 us -> 57.5 us
    pallas_call x1, Pallas kernels: 59.7 us -> 57.5 us  [shards(): pl.pallas_call(functools.partial(kernel, dims), out_shape=jax.ShapeDtypeS...]
where the time goes in v4:
time: 58.7 us; the launch traced here: 58.6 us
  Pallas kernels  57.5 us (98%)
  local copies, waits for them, and re-layouts  1.04 us (2%)
    pallas_call x1, Pallas kernels, shards(): pl.pallas_call(functools.partial(kernel, dims), out_shape=jax.ShapeDtypeS...  57.5 us

profile of v4, /device:TPU:1, one launch (start us, length us, event | category | flops | bytes accessed | tf_op | source)
XLA Modules:
  0.0 58.6 jit_solution(6071046828819375451)
XLA Ops:
  0.0 57.5 %shard_map.46 = f32[19,16,8,128]{3,2,1,0:T(8,128)S(1)} custom-call(s32[1,256]{1,0:T(1,128)} %bitcast.21, s32[4,128]{1,0:T(4,128)} %bitcast.20, f32[19,16,8,128]{3,2,1,0:T(8,128)} %bitcast.18, s32[16,8,128]{2,1,0:T(8,128)} %bitcast.19), custom_call_target="tpu_custom_call" | custom-call | tf_op jit(solution)/shard_map/pallas_call | solution.py:540
  57.5 1.0 %copy.9 = f32[1,4,19,4096]{3,1,2,0:T(4,128)} copy(f32[1,4,19,4096]{3,1,2,0:T(4,128)S(1)} %bitcast.17) | data formatting | bytes 2490368

commit v5 on v4

--- a/solution.py
+++ b/solution.py
@@ -311,19 +311,19 @@
             for f in range(2):
                 table[home + s, f] = stage[chunk, f, pl.ds(s, 8, stride=CAP), :]
 
-    def shift_z(ext, from_below, from_above):
+    def shift_z(ext, from_below, from_above, dirs, start, stop):
         def body(at, carry):
-            for k, i in enumerate(ZPLUS):
-                rim = pltpu.roll(from_below[k], (128 - at) % 128, 1)
-                ext[i, at + 1] = jnp.where(zin == 0, rim, pltpu.roll(ext[i, at + 1], 1, 1))
-            for k, i in enumerate(ZMINUS):
-                rim = pltpu.roll(from_above[k], 15 - at, 1)
-                ext[i, at + 1] = jnp.where(
-                    zin == BE - 1, rim, pltpu.roll(ext[i, at + 1], 127, 1)
-                )
+            for i in dirs:
+                part = ext[i, at + 1]
+                if i in ZPLUS:
+                    rim = pltpu.roll(from_below[ZPLUS.index(i)], (128 - at) % 128, 1)
+                    ext[i, at + 1] = jnp.where(zin == 0, rim, pltpu.roll(part, 1, 1))
+                else:
+                    rim = pltpu.roll(from_above[ZMINUS.index(i)], 15 - at, 1)
+                    ext[i, at + 1] = jnp.where(zin == BE - 1, rim, pltpu.roll(part, 127, 1))
             return carry
 
-        lax.fori_loop(0, BE, body, 0)
+        lax.fori_loop(start, stop, body, 0)
 
     class Gather:
         def __init__(self, table):
@@ -351,11 +351,11 @@
                 self.two[side].wait_recv()
                 self.three[side].start()
             self.four.start()
+
+        def pass_on(self):
             for c in self.one:
                 c.wait_recv()
             self.twin[0].start()
-
-        def pass_on(self):
             for c in self.three:
                 c.wait_recv()
             self.four.wait_recv()
@@ -478,9 +478,13 @@
         second.begin()
         for c in rims:
             c.wait_recv()
-        shift_z(ext, low, high)
+        shift_z(ext, low, high, CHUNKS[2][1], 0, BE)
+        shift_z(ext, low, high, CHUNKS[2][0], 0, 1)
+        shift_z(ext, low, high, CHUNKS[2][0], BE - 1, BE)
         pack(2, ext, tables[2])
         third.begin()
+        shift_z(ext, low, high, CHUNKS[2][0], 1, BE - 1)
+        shift_z(ext, low, high, (5, 6), 0, BE)
         first.forward()
         second.forward()
         third.forward()

time: 58.7 us -> 59 us (level)
  no operation moved by 1% of the time
where the time goes in v5:
time: 59 us; the launch traced here: 58.8 us
  Pallas kernels  57.8 us (98%)
  local copies, waits for them, and re-layouts  1.04 us (2%)
    pallas_call x1, Pallas kernels, shards(): pl.pallas_call(functools.partial(kernel, dims), out_shape=jax.ShapeDtypeS...  57.8 us

profile of v5, /device:TPU:1, one launch (start us, length us, event | category | flops | bytes accessed | tf_op | source)
XLA Modules:
  0.0 58.8 jit_solution(6043329189176079252)
XLA Ops:
  0.0 57.8 %shard_map.46 = f32[19,16,8,128]{3,2,1,0:T(8,128)S(1)} custom-call(s32[1,256]{1,0:T(1,128)} %bitcast.21, s32[4,128]{1,0:T(4,128)} %bitcast.20, f32[19,16,8,128]{3,2,1,0:T(8,128)} %bitcast.18, s32[16,8,128]{2,1,0:T(8,128)} %bitcast.19), custom_call_target="tpu_custom_call" | custom-call | tf_op jit(solution)/shard_map/pallas_call | solution.py:544
  57.8 1.0 %copy.9 = f32[1,4,19,4096]{3,1,2,0:T(4,128)} copy(f32[1,4,19,4096]{3,1,2,0:T(4,128)S(1)} %bitcast.17) | data formatting | bytes 2490368
